TPU v7x, 512 devices: a whole 4x4x16 slice. The times are simulated.
512 devices in a mesh: gz: 8 (over x, core), xy: 64 (over y, z).
Axes of the slice: x: 4, y: 4, z: 16, core: 2. Of those that a mesh axis runs over, the one named last changes fastest.
Arguments:
- pressure_rhs: float32 [64, 2048, 512], P('gz', 'xy'), may hold values from -6 to 6
- inv_density: float32 [64, 2048, 512], P('gz', 'xy'), may hold values from 0.5 to 8
Outputs:
- pressure: float32 [64, 2048, 512], P('gz', 'xy')
- residual: float32 [64, 2048, 512], P('gz', 'xy')
All inputs are finite; a program needn't handle non-finite values.
Results may differ from a plain program's by a relative error of at most 0.0002.
Values sent between devices are 32-bit elements; how exact they have to be, the bound alone decides.
A program may use at most 128 MiB of HBM per device.

v0:
```python
import jax
import jax.numpy as jnp
from jax import lax
from jax.sharding import PartitionSpec as P

LEVELS = 3
SWEEPS = 2
COARSE_SWEEPS = 8


OMEGA = 0.8


def with_halo(cells, sides, width):
    for axis, dim in sides:
        count = lax.axis_size(axis)
        ends = count - 1
        head = lax.slice_in_dim(cells, 0, width, axis=dim)
        tail = lax.slice_in_dim(cells, cells.shape[dim] - width, cells.shape[dim], axis=dim)
        cells = jnp.concatenate(
            [
                lax.ppermute(tail, axis, [(i, (i + 1) % count) for i in range(ends)]),
                cells,
                lax.ppermute(head, axis, [((i + 1) % count, i) for i in range(ends)]),
            ],
            axis=dim,
        )
    return cells


def neighbours(padded):
    return [
        padded[:-2, 1:-1, 1:-1],
        padded[2:, 1:-1, 1:-1],
        padded[1:-1, :-2, 1:-1],
        padded[1:-1, 2:, 1:-1],
        padded[1:-1, 1:-1, :-2],
        padded[1:-1, 1:-1, 2:],
    ]


def face_weights(padded_beta, factor):
    middle = padded_beta[1:-1, 1:-1, 1:-1]
    weights = [0.5 * (middle + beside) for beside in neighbours(padded_beta)]
    diagonal = factor * (
        weights[0] + weights[1] + weights[2] + weights[3] + weights[4] + weights[5]
    )
    return (weights, diagonal)


def apply_operator(values, padded, weights, factor):
    summed = jnp.zeros_like(values)
    for weight, beside in zip(weights, neighbours(padded)):
        summed = summed + weight * (values - beside)
    return factor * summed


def restrict(field):
    z_cells, y_cells, x_cells = field.shape
    return field.reshape(z_cells // 2, 2, y_cells // 2, 2, x_cells // 2, 2).mean(axis=(1, 3, 5))


def prolong(field):
    return jnp.repeat(jnp.repeat(jnp.repeat(field, 2, 0), 2, 1), 2, 2)


def field_faces(values):
    padded = with_halo(values, (("gz", 0), ("xy", 1)), 1)
    return jnp.pad(padded, ((0, 0), (0, 0), (1, 1)))


def density_pad(values):
    padded = with_halo(values, (("gz", 0), ("xy", 1)), 1)
    return jnp.pad(padded, ((0, 0), (0, 0), (1, 1)))


def coarse_pad(values):
    padded = with_halo(values, (("gz", 0), ("xy", 1)), 1)
    return jnp.pad(padded, ((0, 0), (0, 0), (1, 1)))


def smooth(iterate, source, weights, diagonal, factor, repeats, padder):
    for repeat in range(repeats):
        iterate = (
            iterate
            + OMEGA
            * (source - apply_operator(iterate, padder(iterate), weights, factor))
            / diagonal
        )
    return iterate


def shards(pressure_rhs, inv_density):
    top_level = LEVELS
    coefficients = [inv_density]
    for depth_index in range(LEVELS):
        coefficients.append(restrict(coefficients[-1]))
    operators = []
    for depth_index in range(top_level):
        factor = 0.25**depth_index
        weights, diagonal = face_weights(density_pad(coefficients[depth_index]), factor)
        operators.append((weights, diagonal, factor))
    sources = [pressure_rhs]
    smoothed = []
    for depth_index in range(top_level):
        weights, diagonal, factor = operators[depth_index]
        source = sources[depth_index]
        iterate = smooth(
            jnp.zeros_like(source), source, weights, diagonal, factor, SWEEPS, field_faces
        )
        defect = source - apply_operator(iterate, field_faces(iterate), weights, factor)
        smoothed.append(iterate)
        sources.append(restrict(defect))
    top_source = sources[top_level]
    top_beta = coefficients[top_level]
    coarse_factor = 0.25**LEVELS
    weights, diagonal = face_weights(density_pad(top_beta), coarse_factor)
    iterate = smooth(
        jnp.zeros_like(top_source),
        top_source,
        weights,
        diagonal,
        coarse_factor,
        COARSE_SWEEPS,
        coarse_pad,
    )
    for depth_index in reversed(range(top_level)):
        weights, diagonal, factor = operators[depth_index]
        iterate = smoothed[depth_index] + prolong(iterate)
        iterate = smooth(
            iterate, sources[depth_index], weights, diagonal, factor, SWEEPS, field_faces
        )
    weights, diagonal, factor = operators[0]
    residual = pressure_rhs - apply_operator(iterate, field_faces(iterate), weights, factor)
    return (iterate, residual)


def solution(mesh):
    placed = (P("gz", "xy", None), P("gz", "xy", None))
    return jax.shard_map(
        shards,
        mesh=mesh,
        in_specs=placed,
        out_specs=(P("gz", "xy", None), P("gz", "xy", None)),
        check_vma=False,
    )
```

profile of v0, /device:TPU:25, one launch (start us, length us, event | category | flops | bytes accessed | tf_op | source)
XLA Modules:
  0.0 613.7 jit_solution(10840467071283200541)
XLA Ops:
  0.6 3.7 collective-permute-start.1
  6.9 3.6 collective-permute-start.17
  13.3 3.6 collective-permute-start
  17.0 35.6 %reshape.69 = f32[4,2,16,2,256,2]{5,4,3,2,1,0:T(8,128)} reshape(f32[8,32,512]{2,1,0:T(8,128)} %param.3) | data formatting | bytes 1048576 | tf_op jit(solution)/shard_map/reshape | solution.py:60
  52.6 12.2 %reduce_sum.69 = f32[4,16,256]{2,1,0:T(8,128)S(1)} reduce(f32[4,2,16,2,256,2]{5,4,3,2,1,0:T(8,128)} %reshape.69, f32[]{:T(128)} %constant.8.clone.1), dimensions={1,3,5}, to_apply=%region_1.0 | reduce | flops 114688 | bytes 589828 | tf_op jit(solution)/shard_map/reduce_sum | solution.py:60
  66.0 5.6 div.91
  77.7 3.6 collective-permute-done.2
  83.2 3.5 collective-permute-start.4
  86.8 9.7 %collective-permute-start.6 = (f32[10,1,512]{2,1,0:T(1,128)S(1)}, f32[10,1,512]{2,1,0:T(1,128)S(1)}, u32[]{:S(2)}, u32[]{:S(2)}) collective-permute-start(f32[10,1,512]{2,1,0:T(1,128)S(1)} %get-tuple-element.42), channel_id=1, source_target_pairs={{1,0},{2,1},{3,2},{4,3},{5,4},{6,5},{7,6},{8,7},{9,8},{10,9},{11,1... | collective-permute-start | bytes 61448 | tf_op jit(solution)/shard_map/ppermute | solution.py:24
  98.5 5.5 collective-permute-start.7
  104.5 3.2 collective-permute-start.18
  108.4 3.0 collective-permute-start.33
  125.1 5.5 collective-permute-start.11
  133.3 5.5 collective-permute-start.22
  140.0 4.3 collective-permute-start.12
  149.9 4.6 collective-permute-start.23
  156.5 5.5 collective-permute-start.15
  165.5 4.9 collective-permute-start.48
  172.4 35.6 %reshape.68 = f32[4,2,16,2,256,2]{5,4,3,2,1,0:T(8,128)} reshape(f32[8,32,512]{2,1,0:T(8,128)} %fusion.69) | data formatting | bytes 1048576 | tf_op jit(solution)/shard_map/reshape | solution.py:60
  208.0 12.2 %reduce_sum.68 = f32[4,16,256]{2,1,0:T(8,128)S(1)} reduce(f32[4,2,16,2,256,2]{5,4,3,2,1,0:T(8,128)} %reshape.68, f32[]{:T(128)} %constant.8.clone.1), dimensions={1,3,5}, to_apply=%region_0.0 | reduce | flops 114688 | bytes 589828 | tf_op jit(solution)/shard_map/reduce_sum | solution.py:60
  229.7 3.2 collective-permute-start.49
  234.9 5.5 collective-permute-start.27
  243.1 5.5 collective-permute-start.38
  249.6 3.5 collective-permute-start.28
  258.5 5.5 collective-permute-start.39
  265.9 5.5 collective-permute-start.31
  276.4 6.3 %reshape.70 = f32[2,2,8,2,128,2]{5,4,3,2,1,0:T(8,128)} reshape(f32[4,16,256]{2,1,0:T(8,128)} %fusion.175) | data formatting | bytes 131072 | tf_op jit(solution)/shard_map/reshape | solution.py:60
  282.8 3.1 reduce_sum.70
  287.0 4.8 collective-permute-start.40
  296.4 5.5 collective-permute-start.54
  303.8 5.5 collective-permute-start.43
  312.0 5.5 collective-permute-start.55
  318.5 5.3 collective-permute-start.44
  330.7 5.5 collective-permute-start.47
  347.9 3.0 collective-permute-done.57
  352.8 5.9 collective-permute-start.59
  364.9 3.0 collective-permute-done.61
  369.8 6.0 collective-permute-start.63
  382.0 3.0 collective-permute-done.65
  386.9 6.0 collective-permute-start.67
  399.2 3.0 collective-permute-done.69
  404.0 6.0 collective-permute-start.71
  416.3 3.0 collective-permute-done.73
  421.2 6.0 collective-permute-start.75
  433.4 3.0 collective-permute-done.77
  438.3 6.0 collective-permute-start.79
  450.6 3.0 collective-permute-done.81
  455.4 6.0 collective-permute-start.83
  473.3 3.0 collective-permute-done.85
  478.2 6.0 collective-permute-start.87
  485.9 2.8 collective-permute-start.88
  490.7 3.0 collective-permute-done.89
  495.6 6.0 collective-permute-start.91
  514.9 3.1 collective-permute-done.93
  520.0 6.0 collective-permute-start.95
  532.7 3.1 collective-permute-done.97
  538.0 6.0 collective-permute-start.99
  553.4 3.0 copy.250
  562.4 3.6 collective-permute-done.101
  568.0 6.0 collective-permute-start.103
  580.8 3.6 collective-permute-done.105
  586.4 6.0 collective-permute-start.107
  599.3 3.6 collective-permute-done.109
  604.9 6.0 collective-permute-start.111
  (360 shorter events, 235.9 us)
Async XLA Ops:
  0.6 82.6 %collective-permute-start.1 = (f32[1,32,512]{2,1,0:T(8,128)S(1)}, f32[1,32,512]{2,1,0:T(8,128)S(1)}, u32[]{:S(2)}, u32[]{:S(2)}) collective-permute-start(f32[1,32,512]{2,1,0:T(8,128)S(1)} %broadcast.158), channel_id=1, source_target_pairs={{0,64},{64,128},{128,192},{192,256},{256,320},{320,384},{384,448},... | collective-permute-start | bytes 196616 | tf_op jit(solution)/shard_map/ppermute | solution.py:22
  4.3 82.5 %collective-permute-start.3 = (f32[1,32,512]{2,1,0:T(8,128)S(1)}, f32[1,32,512]{2,1,0:T(8,128)S(1)}, u32[]{:S(2)}, u32[]{:S(2)}) collective-permute-start(f32[1,32,512]{2,1,0:T(8,128)S(1)} %broadcast.158), channel_id=1, source_target_pairs={{64,0},{128,64},{192,128},{256,192},{320,256},{384,320},{448,384},... | collective-permute-start | bytes 196616 | tf_op jit(solution)/shard_map/ppermute | solution.py:24
  6.9 116.3 %collective-permute-start.17 = (f32[1,16,256]{2,1,0:T(8,128)}, f32[1,16,256]{2,1,0:T(8,128)}, u32[]{:S(2)}, u32[]{:S(2)}) collective-permute-start(f32[1,16,256]{2,1,0:T(8,128)} %broadcast.162), channel_id=1, source_target_pairs={{0,64},{64,128},{128,192},{192,256},{256,320},{320,384},{384,448},... | collective-permute-start | bytes 49160 | tf_op jit(solution)/shard_map/ppermute | solution.py:22
  10.5 114.6 %collective-permute-start.19 = (f32[1,16,256]{2,1,0:T(8,128)}, f32[1,16,256]{2,1,0:T(8,128)}, u32[]{:S(2)}, u32[]{:S(2)}) collective-permute-start(f32[1,16,256]{2,1,0:T(8,128)} %broadcast.162), channel_id=1, source_target_pairs={{64,0},{128,64},{192,128},{256,192},{320,256},{384,320},{448,384},... | collective-permute-start | bytes 49160 | tf_op jit(solution)/shard_map/ppermute | solution.py:24
  13.3 62.4 %collective-permute-start = (f32[1,32,512]{2,1,0:T(8,128)S(1)}, f32[1,32,512]{2,1,0:T(8,128)S(1)}, u32[]{:S(2)}, u32[]{:S(2)}) collective-permute-start(f32[1,32,512]{2,1,0:T(8,128)S(1)} %get-tuple-element.57), channel_id=1, source_target_pairs={{0,64},{64,128},{128,192},{192,256},{256,320},{320,384},{384,448},... | collective-permute-start | bytes 196616 | tf_op jit(solution)/shard_map/ppermute | solution.py:22
  81.3 31.8 %collective-permute-start.16 = (f32[1,16,256]{2,1,0:T(8,128)}, f32[1,16,256]{2,1,0:T(8,128)S(1)}, u32[]{:S(2)}, u32[]{:S(2)}) collective-permute-start(f32[1,16,256]{2,1,0:T(8,128)} %get-tuple-element.79), channel_id=1, source_target_pairs={{0,64},{64,128},{128,192},{192,256},{256,320},{320,384},{384,448},... | collective-permute-start | bytes 49160 | tf_op jit(solution)/shard_map/ppermute | solution.py:22
  83.2 13.4 %collective-permute-start.4 = (f32[10,1,512]{2,1,0:T(1,128)S(1)}, f32[10,1,512]{2,1,0:T(1,128)S(1)}, u32[]{:S(2)}, u32[]{:S(2)}) collective-permute-start(f32[10,1,512]{2,1,0:T(1,128)S(1)} %get-tuple-element.43), channel_id=1, source_target_pairs={{0,1},{1,2},{2,3},{3,4},{4,5},{5,6},{6,7},{7,8},{8,9},{9,10},{10,1... | collective-permute-start | bytes 61448 | tf_op jit(solution)/shard_map/ppermute | solution.py:22
  86.8 11.7 %collective-permute-start.6 = (f32[10,1,512]{2,1,0:T(1,128)S(1)}, f32[10,1,512]{2,1,0:T(1,128)S(1)}, u32[]{:S(2)}, u32[]{:S(2)}) collective-permute-start(f32[10,1,512]{2,1,0:T(1,128)S(1)} %get-tuple-element.42), channel_id=1, source_target_pairs={{1,0},{2,1},{3,2},{4,3},{5,4},{6,5},{7,6},{8,7},{9,8},{10,9},{11,1... | collective-permute-start | bytes 61448 | tf_op jit(solution)/shard_map/ppermute | solution.py:24
  96.6 7.9 %collective-permute-start.5 = (f32[10,1,512]{2,1,0:T(1,128)S(1)}, f32[10,1,512]{2,1,0:T(1,128)S(1)}, u32[]{:S(2)}, u32[]{:S(2)}) collective-permute-start(f32[10,1,512]{2,1,0:T(1,128)S(1)} %get-tuple-element.44), channel_id=1, source_target_pairs={{0,1},{1,2},{2,3},{3,4},{4,5},{5,6},{6,7},{7,8},{8,9},{9,10},{10,1... | collective-permute-start | bytes 61448 | tf_op jit(solution)/shard_map/ppermute | solution.py:22
  98.5 9.2 %collective-permute-start.7 = (f32[10,1,512]{2,1,0:T(1,128)S(1)}, f32[10,1,512]{2,1,0:T(1,128)S(1)}, u32[]{:S(2)}, u32[]{:S(2)}) collective-permute-start(f32[10,1,512]{2,1,0:T(1,128)S(1)} %get-tuple-element.45), channel_id=1, source_target_pairs={{1,0},{2,1},{3,2},{4,3},{5,4},{6,5},{7,6},{8,7},{9,8},{10,9},{11,1... | collective-permute-start | bytes 61448 | tf_op jit(solution)/shard_map/ppermute | solution.py:24
  104.5 11.0 %collective-permute-start.18 = (f32[1,16,256]{2,1,0:T(8,128)}, f32[1,16,256]{2,1,0:T(8,128)S(1)}, u32[]{:S(2)}, u32[]{:S(2)}) collective-permute-start(f32[1,16,256]{2,1,0:T(8,128)} %get-tuple-element.78), channel_id=1, source_target_pairs={{64,0},{128,64},{192,128},{256,192},{320,256},{384,320},{448,384},... | collective-permute-start | bytes 49160 | tf_op jit(solution)/shard_map/ppermute | solution.py:24
  108.4 124.6 %collective-permute-start.33 = (f32[1,8,128]{2,1,0:T(8,128)}, f32[1,8,128]{2,1,0:T(8,128)}, u32[]{:S(2)}, u32[]{:S(2)}) collective-permute-start(f32[1,8,128]{2,1,0:T(8,128)} %broadcast.167), channel_id=1, source_target_pairs={{0,64},{64,128},{128,192},{192,256},{256,320},{320,384},{384,448},... | collective-permute-start | bytes 12296 | tf_op jit(solution)/shard_map/ppermute | solution.py:22
  117.5 117.4 %collective-permute-start.35 = (f32[1,8,128]{2,1,0:T(8,128)}, f32[1,8,128]{2,1,0:T(8,128)}, u32[]{:S(2)}, u32[]{:S(2)}) collective-permute-start(f32[1,8,128]{2,1,0:T(8,128)} %broadcast.167), channel_id=1, source_target_pairs={{64,0},{128,64},{192,128},{256,192},{320,256},{384,320},{448,384},... | collective-permute-start | bytes 12296 | tf_op jit(solution)/shard_map/ppermute | solution.py:24
  121.1 100.5 %collective-permute-start.32 = (f32[1,8,128]{2,1,0:T(8,128)}, f32[1,8,128]{2,1,0:T(8,128)}, u32[]{:S(2)}, u32[]{:S(2)}) collective-permute-start(f32[1,8,128]{2,1,0:T(8,128)} %get-tuple-element.103), channel_id=1, source_target_pairs={{0,64},{64,128},{128,192},{192,256},{256,320},{320,384},{384,448},... | collective-permute-start | bytes 12296 | tf_op jit(solution)/shard_map/ppermute | solution.py:22
  123.1 8.2 %collective-permute-start.10 = (f32[10,1,512]{2,1,0:T(1,128)S(1)}, f32[10,1,512]{2,1,0:T(1,128)S(1)}, u32[]{:S(2)}, u32[]{:S(2)}) collective-permute-start(f32[10,1,512]{2,1,0:T(1,128)S(1)} %get-tuple-element.40), channel_id=1, source_target_pairs={{0,1},{1,2},{2,3},{3,4},{4,5},{5,6},{6,7},{7,8},{8,9},{9,10},{10,1... | collective-permute-start | bytes 61448 | tf_op jit(solution)/shard_map/ppermute | solution.py:22
  125.1 8.2 %collective-permute-start.11 = (f32[10,1,512]{2,1,0:T(1,128)S(1)}, f32[10,1,512]{2,1,0:T(1,128)S(1)}, u32[]{:S(2)}, u32[]{:S(2)}) collective-permute-start(f32[10,1,512]{2,1,0:T(1,128)S(1)} %get-tuple-element.41), channel_id=1, source_target_pairs={{1,0},{2,1},{3,2},{4,3},{5,4},{6,5},{7,6},{8,7},{9,8},{10,9},{11,1... | collective-permute-start | bytes 61448 | tf_op jit(solution)/shard_map/ppermute | solution.py:24
  131.3 8.7 %collective-permute-start.20 = (f32[6,1,256]{2,1,0:T(1,128)S(1)}, f32[6,1,256]{2,1,0:T(1,128)S(1)}, u32[]{:S(2)}, u32[]{:S(2)}) collective-permute-start(f32[6,1,256]{2,1,0:T(1,128)S(1)} %get-tuple-element.67), channel_id=1, source_target_pairs={{0,1},{1,2},{2,3},{3,4},{4,5},{5,6},{6,7},{7,8},{8,9},{9,10},{10,1... | collective-permute-start | bytes 18440 | tf_op jit(solution)/shard_map/ppermute | solution.py:22
  133.3 11.0 %collective-permute-start.22 = (f32[6,1,256]{2,1,0:T(1,128)S(1)}, f32[6,1,256]{2,1,0:T(1,128)S(1)}, u32[]{:S(2)}, u32[]{:S(2)}) collective-permute-start(f32[6,1,256]{2,1,0:T(1,128)S(1)} %get-tuple-element.66), channel_id=1, source_target_pairs={{1,0},{2,1},{3,2},{4,3},{5,4},{6,5},{7,6},{8,7},{9,8},{10,9},{11,1... | collective-permute-start | bytes 18440 | tf_op jit(solution)/shard_map/ppermute | solution.py:24
  140.0 7.1 %collective-permute-start.12 = (f32[1,32,512]{2,1,0:T(8,128)S(1)}, f32[1,32,512]{2,1,0:T(8,128)S(1)}, u32[]{:S(2)}, u32[]{:S(2)}) collective-permute-start(f32[1,32,512]{2,1,0:T(8,128)S(1)} %get-tuple-element.52), channel_id=1, source_target_pairs={{0,64},{64,128},{128,192},{192,256},{256,320},{320,384},{384,448},... | collective-permute-start | bytes 196616 | tf_op jit(solution)/shard_map/ppermute | solution.py:22
  147.1 7.5 %collective-permute-start.21 = (f32[6,1,256]{2,1,0:T(1,128)S(1)}, f32[6,1,256]{2,1,0:T(1,128)S(1)}, u32[]{:S(2)}, u32[]{:S(2)}) collective-permute-start(f32[6,1,256]{2,1,0:T(1,128)S(1)} %get-tuple-element.68), channel_id=1, source_target_pairs={{0,1},{1,2},{2,3},{3,4},{4,5},{5,6},{6,7},{7,8},{8,9},{9,10},{10,1... | collective-permute-start | bytes 18440 | tf_op jit(solution)/shard_map/ppermute | solution.py:22
  154.6 9.0 %collective-permute-start.14 = (f32[10,1,512]{2,1,0:T(1,128)S(1)}, f32[10,1,512]{2,1,0:T(1,128)S(1)}, u32[]{:S(2)}, u32[]{:S(2)}) collective-permute-start(f32[10,1,512]{2,1,0:T(1,128)S(1)} %get-tuple-element.38), channel_id=1, source_target_pairs={{0,1},{1,2},{2,3},{3,4},{4,5},{5,6},{6,7},{7,8},{8,9},{9,10},{10,1... | collective-permute-start | bytes 61448 | tf_op jit(solution)/shard_map/ppermute | solution.py:22
  156.5 9.0 %collective-permute-start.15 = (f32[10,1,512]{2,1,0:T(1,128)S(1)}, f32[10,1,512]{2,1,0:T(1,128)S(1)}, u32[]{:S(2)}, u32[]{:S(2)}) collective-permute-start(f32[10,1,512]{2,1,0:T(1,128)S(1)} %get-tuple-element.39), channel_id=1, source_target_pairs={{1,0},{2,1},{3,2},{4,3},{5,4},{6,5},{7,6},{8,7},{9,8},{10,9},{11,1... | collective-permute-start | bytes 61448 | tf_op jit(solution)/shard_map/ppermute | solution.py:24
  163.6 60.4 %collective-permute-start.34 = (f32[1,8,128]{2,1,0:T(8,128)}, f32[1,8,128]{2,1,0:T(8,128)}, u32[]{:S(2)}, u32[]{:S(2)}) collective-permute-start(f32[1,8,128]{2,1,0:T(8,128)} %get-tuple-element.102), channel_id=1, source_target_pairs={{64,0},{128,64},{192,128},{256,192},{320,256},{384,320},{448,384},... | collective-permute-start | bytes 12296 | tf_op jit(solution)/shard_map/ppermute | solution.py:24
  165.5 126.2 %collective-permute-start.48 = (f32[1,4,64]{2,1,0:T(4,128)}, f32[1,4,64]{2,1,0:T(4,128)}, u32[]{:S(2)}, u32[]{:S(2)}) collective-permute-start(f32[1,4,64]{2,1,0:T(4,128)} %multiply_bitcast_fusion), channel_id=1, source_target_pairs={{0,64},{64,128},{128,192},{192,256},{256,320},{320,384},{384,448},... | collective-permute-start | bytes 3080 | tf_op jit(solution)/shard_map/ppermute | solution.py:22
  226.8 66.9 %collective-permute-start.50 = (f32[1,4,64]{2,1,0:T(4,128)}, f32[1,4,64]{2,1,0:T(4,128)}, u32[]{:S(2)}, u32[]{:S(2)}) collective-permute-start(f32[1,4,64]{2,1,0:T(4,128)} %multiply_bitcast_fusion), channel_id=1, source_target_pairs={{64,0},{128,64},{192,128},{256,192},{320,256},{384,320},{448,384},... | collective-permute-start | bytes 3080 | tf_op jit(solution)/shard_map/ppermute | solution.py:24
  229.7 74.1 %collective-permute-start.49 = (f32[1,4,64]{2,1,0:T(4,128)}, f32[1,4,64]{2,1,0:T(4,128)}, u32[]{:S(2)}, u32[]{:S(2)}) collective-permute-start(f32[1,4,64]{2,1,0:T(4,128)} %broadcast_in_dim.46), channel_id=1, source_target_pairs={{0,64},{64,128},{128,192},{192,256},{256,320},{320,384},{384,448},... | collective-permute-start | bytes 3080 | tf_op jit(solution)/shard_map/ppermute | solution.py:22
  233.0 8.2 %collective-permute-start.26 = (f32[6,1,256]{2,1,0:T(1,128)S(1)}, f32[6,1,256]{2,1,0:T(1,128)S(1)}, u32[]{:S(2)}, u32[]{:S(2)}) collective-permute-start(f32[6,1,256]{2,1,0:T(1,128)S(1)} %get-tuple-element.64), channel_id=1, source_target_pairs={{0,1},{1,2},{2,3},{3,4},{4,5},{5,6},{6,7},{7,8},{8,9},{9,10},{10,1... | collective-permute-start | bytes 18440 | tf_op jit(solution)/shard_map/ppermute | solution.py:22
  234.9 8.2 %collective-permute-start.27 = (f32[6,1,256]{2,1,0:T(1,128)S(1)}, f32[6,1,256]{2,1,0:T(1,128)S(1)}, u32[]{:S(2)}, u32[]{:S(2)}) collective-permute-start(f32[6,1,256]{2,1,0:T(1,128)S(1)} %get-tuple-element.65), channel_id=1, source_target_pairs={{1,0},{2,1},{3,2},{4,3},{5,4},{6,5},{7,6},{8,7},{9,8},{10,9},{11,1... | collective-permute-start | bytes 18440 | tf_op jit(solution)/shard_map/ppermute | solution.py:24
  241.2 8.4 %collective-permute-start.36 = (f32[4,1,128]{2,1,0:T(1,128)S(1)}, f32[4,1,128]{2,1,0:T(1,128)S(1)}, u32[]{:S(2)}, u32[]{:S(2)}) collective-permute-start(f32[4,1,128]{2,1,0:T(1,128)S(1)} %get-tuple-element.89), channel_id=1, source_target_pairs={{0,1},{1,2},{2,3},{3,4},{4,5},{5,6},{6,7},{7,8},{8,9},{9,10},{10,1... | collective-permute-start | bytes 6152 | tf_op jit(solution)/shard_map/ppermute | solution.py:22
  243.1 10.1 %collective-permute-start.38 = (f32[4,1,128]{2,1,0:T(1,128)S(1)}, f32[4,1,128]{2,1,0:T(1,128)S(1)}, u32[]{:S(2)}, u32[]{:S(2)}) collective-permute-start(f32[4,1,128]{2,1,0:T(1,128)S(1)} %get-tuple-element.88), channel_id=1, source_target_pairs={{1,0},{2,1},{3,2},{4,3},{5,4},{6,5},{7,6},{8,7},{9,8},{10,9},{11,1... | collective-permute-start | bytes 6152 | tf_op jit(solution)/shard_map/ppermute | solution.py:24
  249.6 6.9 %collective-permute-start.28 = (f32[1,16,256]{2,1,0:T(8,128)S(1)}, f32[1,16,256]{2,1,0:T(8,128)S(1)}, u32[]{:S(2)}, u32[]{:S(2)}) collective-permute-start(f32[1,16,256]{2,1,0:T(8,128)S(1)} %get-tuple-element.74), channel_id=1, source_target_pairs={{0,64},{64,128},{128,192},{192,256},{256,320},{320,384},{384,448},... | collective-permute-start | bytes 49160 | tf_op jit(solution)/shard_map/ppermute | solution.py:22
  256.5 7.4 %collective-permute-start.37 = (f32[4,1,128]{2,1,0:T(1,128)S(1)}, f32[4,1,128]{2,1,0:T(1,128)S(1)}, u32[]{:S(2)}, u32[]{:S(2)}) collective-permute-start(f32[4,1,128]{2,1,0:T(1,128)S(1)} %get-tuple-element.90), channel_id=1, source_target_pairs={{0,1},{1,2},{2,3},{3,4},{4,5},{5,6},{6,7},{7,8},{8,9},{9,10},{10,1... | collective-permute-start | bytes 6152 | tf_op jit(solution)/shard_map/ppermute | solution.py:22
  258.5 7.5 %collective-permute-start.39 = (f32[4,1,128]{2,1,0:T(1,128)S(1)}, f32[4,1,128]{2,1,0:T(1,128)S(1)}, u32[]{:S(2)}, u32[]{:S(2)}) collective-permute-start(f32[4,1,128]{2,1,0:T(1,128)S(1)} %get-tuple-element.91), channel_id=1, source_target_pairs={{1,0},{2,1},{3,2},{4,3},{5,4},{6,5},{7,6},{8,7},{9,8},{10,9},{11,1... | collective-permute-start | bytes 6152 | tf_op jit(solution)/shard_map/ppermute | solution.py:24
  264.0 8.9 %collective-permute-start.30 = (f32[6,1,256]{2,1,0:T(1,128)S(1)}, f32[6,1,256]{2,1,0:T(1,128)S(1)}, u32[]{:S(2)}, u32[]{:S(2)}) collective-permute-start(f32[6,1,256]{2,1,0:T(1,128)S(1)} %get-tuple-element.62), channel_id=1, source_target_pairs={{0,1},{1,2},{2,3},{3,4},{4,5},{5,6},{6,7},{7,8},{8,9},{9,10},{10,1... | collective-permute-start | bytes 18440 | tf_op jit(solution)/shard_map/ppermute | solution.py:22
  265.9 8.8 %collective-permute-start.31 = (f32[6,1,256]{2,1,0:T(1,128)S(1)}, f32[6,1,256]{2,1,0:T(1,128)S(1)}, u32[]{:S(2)}, u32[]{:S(2)}) collective-permute-start(f32[6,1,256]{2,1,0:T(1,128)S(1)} %get-tuple-element.63), channel_id=1, source_target_pairs={{1,0},{2,1},{3,2},{4,3},{5,4},{6,5},{7,6},{8,7},{9,8},{10,9},{11,1... | collective-permute-start | bytes 18440 | tf_op jit(solution)/shard_map/ppermute | solution.py:24
  272.8 36.5 %collective-permute-start.51 = (f32[1,4,64]{2,1,0:T(4,128)}, f32[1,4,64]{2,1,0:T(4,128)}, u32[]{:S(2)}, u32[]{:S(2)}) collective-permute-start(f32[1,4,64]{2,1,0:T(4,128)} %broadcast_in_dim.46), channel_id=1, source_target_pairs={{64,0},{128,64},{192,128},{256,192},{320,256},{384,320},{448,384},... | collective-permute-start | bytes 3080 | tf_op jit(solution)/shard_map/ppermute | solution.py:24
  287.0 9.4 %collective-permute-start.40 = (f32[1,8,128]{2,1,0:T(8,128)S(1)}, f32[1,8,128]{2,1,0:T(8,128)S(1)}, u32[]{:S(2)}, u32[]{:S(2)}) collective-permute-start(f32[1,8,128]{2,1,0:T(8,128)S(1)} %get-tuple-element.100), channel_id=1, source_target_pairs={{0,64},{64,128},{128,192},{192,256},{256,320},{320,384},{384,448},... | collective-permute-start | bytes 12296 | tf_op jit(solution)/shard_map/ppermute | solution.py:22
  291.8 10.1 %collective-permute-start.41 = (f32[1,8,128]{2,1,0:T(8,128)S(1)}, f32[1,8,128]{2,1,0:T(8,128)S(1)}, u32[]{:S(2)}, u32[]{:S(2)}) collective-permute-start(f32[1,8,128]{2,1,0:T(8,128)S(1)} %get-tuple-element.101), channel_id=1, source_target_pairs={{64,0},{128,64},{192,128},{256,192},{320,256},{384,320},{448,384},... | collective-permute-start | bytes 12296 | tf_op jit(solution)/shard_map/ppermute | solution.py:24
  294.5 29.4 %collective-permute-start.52 = (f32[3,1,64]{2,1,0:T(1,128)S(1)}, f32[3,1,64]{2,1,0:T(1,128)S(1)}, u32[]{:S(2)}, u32[]{:S(2)}) collective-permute-start(f32[3,1,64]{2,1,0:T(1,128)S(1)} %get-tuple-element.119), channel_id=1, source_target_pairs={{0,1},{1,2},{2,3},{3,4},{4,5},{5,6},{6,7},{7,8},{8,9},{9,10},{10,1... | collective-permute-start | bytes 2312 | tf_op jit(solution)/shard_map/ppermute | solution.py:22
  296.4 29.4 %collective-permute-start.54 = (f32[3,1,64]{2,1,0:T(1,128)S(1)}, f32[3,1,64]{2,1,0:T(1,128)S(1)}, u32[]{:S(2)}, u32[]{:S(2)}) collective-permute-start(f32[3,1,64]{2,1,0:T(1,128)S(1)} %get-tuple-element.118), channel_id=1, source_target_pairs={{1,0},{2,1},{3,2},{4,3},{5,4},{6,5},{7,6},{8,7},{9,8},{10,9},{11,1... | collective-permute-start | bytes 2312 | tf_op jit(solution)/shard_map/ppermute | solution.py:24
  301.9 10.1 %collective-permute-start.42 = (f32[4,1,128]{2,1,0:T(1,128)S(1)}, f32[4,1,128]{2,1,0:T(1,128)S(1)}, u32[]{:S(2)}, u32[]{:S(2)}) collective-permute-start(f32[4,1,128]{2,1,0:T(1,128)S(1)} %get-tuple-element.86), channel_id=1, source_target_pairs={{0,1},{1,2},{2,3},{3,4},{4,5},{5,6},{6,7},{7,8},{8,9},{9,10},{10,1... | collective-permute-start | bytes 6152 | tf_op jit(solution)/shard_map/ppermute | solution.py:22
  303.8 13.7 %collective-permute-start.43 = (f32[4,1,128]{2,1,0:T(1,128)S(1)}, f32[4,1,128]{2,1,0:T(1,128)S(1)}, u32[]{:S(2)}, u32[]{:S(2)}) collective-permute-start(f32[4,1,128]{2,1,0:T(1,128)S(1)} %get-tuple-element.87), channel_id=1, source_target_pairs={{1,0},{2,1},{3,2},{4,3},{5,4},{6,5},{7,6},{8,7},{9,8},{10,9},{11,1... | collective-permute-start | bytes 6152 | tf_op jit(solution)/shard_map/ppermute | solution.py:24
  310.1 26.1 %collective-permute-start.53 = (f32[3,1,64]{2,1,0:T(1,128)S(1)}, f32[3,1,64]{2,1,0:T(1,128)S(1)}, u32[]{:S(2)}, u32[]{:S(2)}) collective-permute-start(f32[3,1,64]{2,1,0:T(1,128)S(1)} %get-tuple-element.120), channel_id=1, source_target_pairs={{0,1},{1,2},{2,3},{3,4},{4,5},{5,6},{6,7},{7,8},{8,9},{9,10},{10,1... | collective-permute-start | bytes 2312 | tf_op jit(solution)/shard_map/ppermute | solution.py:22
  312.0 24.2 %collective-permute-start.55 = (f32[3,1,64]{2,1,0:T(1,128)S(1)}, f32[3,1,64]{2,1,0:T(1,128)S(1)}, u32[]{:S(2)}, u32[]{:S(2)}) collective-permute-start(f32[3,1,64]{2,1,0:T(1,128)S(1)} %get-tuple-element.121), channel_id=1, source_target_pairs={{1,0},{2,1},{3,2},{4,3},{5,4},{6,5},{7,6},{8,7},{9,8},{10,9},{11,1... | collective-permute-start | bytes 2312 | tf_op jit(solution)/shard_map/ppermute | solution.py:24
  318.5 8.7 %collective-permute-start.44 = (f32[1,8,128]{2,1,0:T(8,128)S(1)}, f32[1,8,128]{2,1,0:T(8,128)S(1)}, u32[]{:S(2)}, u32[]{:S(2)}) collective-permute-start(f32[1,8,128]{2,1,0:T(8,128)S(1)} %get-tuple-element.98), channel_id=1, source_target_pairs={{0,64},{64,128},{128,192},{192,256},{256,320},{320,384},{384,448},... | collective-permute-start | bytes 12296 | tf_op jit(solution)/shard_map/ppermute | solution.py:22
  328.8 8.8 %collective-permute-start.46 = (f32[4,1,128]{2,1,0:T(1,128)S(1)}, f32[4,1,128]{2,1,0:T(1,128)S(1)}, u32[]{:S(2)}, u32[]{:S(2)}) collective-permute-start(f32[4,1,128]{2,1,0:T(1,128)S(1)} %get-tuple-element.84), channel_id=1, source_target_pairs={{0,1},{1,2},{2,3},{3,4},{4,5},{5,6},{6,7},{7,8},{8,9},{9,10},{10,1... | collective-permute-start | bytes 6152 | tf_op jit(solution)/shard_map/ppermute | solution.py:22
  330.7 6.9 %collective-permute-start.47 = (f32[4,1,128]{2,1,0:T(1,128)S(1)}, f32[4,1,128]{2,1,0:T(1,128)S(1)}, u32[]{:S(2)}, u32[]{:S(2)}) collective-permute-start(f32[4,1,128]{2,1,0:T(1,128)S(1)} %get-tuple-element.85), channel_id=1, source_target_pairs={{1,0},{2,1},{3,2},{4,3},{5,4},{6,5},{7,6},{8,7},{9,8},{10,9},{11,1... | collective-permute-start | bytes 6152 | tf_op jit(solution)/shard_map/ppermute | solution.py:24
  350.9 7.8 %collective-permute-start.58 = (f32[3,1,64]{2,1,0:T(1,128)S(1)}, f32[3,1,64]{2,1,0:T(1,128)S(1)}, u32[]{:S(2)}, u32[]{:S(2)}) collective-permute-start(f32[3,1,64]{2,1,0:T(1,128)S(1)} %get-tuple-element.116), channel_id=1, source_target_pairs={{0,1},{1,2},{2,3},{3,4},{4,5},{5,6},{6,7},{7,8},{8,9},{9,10},{10,1... | collective-permute-start | bytes 2312 | tf_op jit(solution)/shard_map/ppermute | solution.py:22
  367.9 7.9 %collective-permute-start.62 = (f32[3,1,64]{2,1,0:T(1,128)S(1)}, f32[3,1,64]{2,1,0:T(1,128)S(1)}, u32[]{:S(2)}, u32[]{:S(2)}) collective-permute-start(f32[3,1,64]{2,1,0:T(1,128)S(1)} %get-tuple-element.114), channel_id=1, source_target_pairs={{0,1},{1,2},{2,3},{3,4},{4,5},{5,6},{6,7},{7,8},{8,9},{9,10},{10,1... | collective-permute-start | bytes 2312 | tf_op jit(solution)/shard_map/ppermute | solution.py:22
  385.0 7.9 %collective-permute-start.66 = (f32[3,1,64]{2,1,0:T(1,128)S(1)}, f32[3,1,64]{2,1,0:T(1,128)S(1)}, u32[]{:S(2)}, u32[]{:S(2)}) collective-permute-start(f32[3,1,64]{2,1,0:T(1,128)S(1)} %get-tuple-element.112), channel_id=1, source_target_pairs={{0,1},{1,2},{2,3},{3,4},{4,5},{5,6},{6,7},{7,8},{8,9},{9,10},{10,1... | collective-permute-start | bytes 2312 | tf_op jit(solution)/shard_map/ppermute | solution.py:22
  402.1 7.9 %collective-permute-start.70 = (f32[3,1,64]{2,1,0:T(1,128)S(1)}, f32[3,1,64]{2,1,0:T(1,128)S(1)}, u32[]{:S(2)}, u32[]{:S(2)}) collective-permute-start(f32[3,1,64]{2,1,0:T(1,128)S(1)} %get-tuple-element.110), channel_id=1, source_target_pairs={{0,1},{1,2},{2,3},{3,4},{4,5},{5,6},{6,7},{7,8},{8,9},{9,10},{10,1... | collective-permute-start | bytes 2312 | tf_op jit(solution)/shard_map/ppermute | solution.py:22
  419.3 7.9 %collective-permute-start.74 = (f32[3,1,64]{2,1,0:T(1,128)S(1)}, f32[3,1,64]{2,1,0:T(1,128)S(1)}, u32[]{:S(2)}, u32[]{:S(2)}) collective-permute-start(f32[3,1,64]{2,1,0:T(1,128)S(1)} %get-tuple-element.108), channel_id=1, source_target_pairs={{0,1},{1,2},{2,3},{3,4},{4,5},{5,6},{6,7},{7,8},{8,9},{9,10},{10,1... | collective-permute-start | bytes 2312 | tf_op jit(solution)/shard_map/ppermute | solution.py:22
  436.4 7.9 %collective-permute-start.78 = (f32[3,1,64]{2,1,0:T(1,128)S(1)}, f32[3,1,64]{2,1,0:T(1,128)S(1)}, u32[]{:S(2)}, u32[]{:S(2)}) collective-permute-start(f32[3,1,64]{2,1,0:T(1,128)S(1)} %get-tuple-element.106), channel_id=1, source_target_pairs={{0,1},{1,2},{2,3},{3,4},{4,5},{5,6},{6,7},{7,8},{8,9},{9,10},{10,1... | collective-permute-start | bytes 2312 | tf_op jit(solution)/shard_map/ppermute | solution.py:22
  453.5 7.9 %collective-permute-start.82 = (f32[3,1,64]{2,1,0:T(1,128)S(1)}, f32[3,1,64]{2,1,0:T(1,128)S(1)}, u32[]{:S(2)}, u32[]{:S(2)}) collective-permute-start(f32[3,1,64]{2,1,0:T(1,128)S(1)} %get-tuple-element.104), channel_id=1, source_target_pairs={{0,1},{1,2},{2,3},{3,4},{4,5},{5,6},{6,7},{7,8},{8,9},{9,10},{10,1... | collective-permute-start | bytes 2312 | tf_op jit(solution)/shard_map/ppermute | solution.py:22
  476.2 7.9 %collective-permute-start.86 = (f32[4,1,128]{2,1,0:T(1,128)S(1)}, f32[4,1,128]{2,1,0:T(1,128)S(1)}, u32[]{:S(2)}, u32[]{:S(2)}) collective-permute-start(f32[4,1,128]{2,1,0:T(1,128)S(1)} %get-tuple-element.82), channel_id=1, source_target_pairs={{0,1},{1,2},{2,3},{3,4},{4,5},{5,6},{6,7},{7,8},{8,9},{9,10},{10,1... | collective-permute-start | bytes 6152 | tf_op jit(solution)/shard_map/ppermute | solution.py:22
  493.7 7.9 %collective-permute-start.90 = (f32[4,1,128]{2,1,0:T(1,128)S(1)}, f32[4,1,128]{2,1,0:T(1,128)S(1)}, u32[]{:S(2)}, u32[]{:S(2)}) collective-permute-start(f32[4,1,128]{2,1,0:T(1,128)S(1)} %get-tuple-element.80), channel_id=1, source_target_pairs={{0,1},{1,2},{2,3},{3,4},{4,5},{5,6},{6,7},{7,8},{8,9},{9,10},{10,1... | collective-permute-start | bytes 6152 | tf_op jit(solution)/shard_map/ppermute | solution.py:22
  518.0 8.0 %collective-permute-start.94 = (f32[6,1,256]{2,1,0:T(1,128)S(1)}, f32[6,1,256]{2,1,0:T(1,128)S(1)}, u32[]{:S(2)}, u32[]{:S(2)}) collective-permute-start(f32[6,1,256]{2,1,0:T(1,128)S(1)} %get-tuple-element.60), channel_id=1, source_target_pairs={{0,1},{1,2},{2,3},{3,4},{4,5},{5,6},{6,7},{7,8},{8,9},{9,10},{10,1... | collective-permute-start | bytes 18440 | tf_op jit(solution)/shard_map/ppermute | solution.py:22
  535.8 8.2 %collective-permute-start.98 = (f32[6,1,256]{2,1,0:T(1,128)S(1)}, f32[6,1,256]{2,1,0:T(1,128)S(1)}, u32[]{:S(2)}, u32[]{:S(2)}) collective-permute-start(f32[6,1,256]{2,1,0:T(1,128)S(1)} %get-tuple-element.58), channel_id=1, source_target_pairs={{0,1},{1,2},{2,3},{3,4},{4,5},{5,6},{6,7},{7,8},{8,9},{9,10},{10,1... | collective-permute-start | bytes 18440 | tf_op jit(solution)/shard_map/ppermute | solution.py:22
  566.1 8.0 %collective-permute-start.102 = (f32[10,1,512]{2,1,0:T(1,128)S(1)}, f32[10,1,512]{2,1,0:T(1,128)S(1)}, u32[]{:S(2)}, u32[]{:S(2)}) collective-permute-start(f32[10,1,512]{2,1,0:T(1,128)S(1)} %get-tuple-element.36), channel_id=1, source_target_pairs={{0,1},{1,2},{2,3},{3,4},{4,5},{5,6},{6,7},{7,8},{8,9},{9,10},{10,1... | collective-permute-start | bytes 61448 | tf_op jit(solution)/shard_map/ppermute | solution.py:22
  568.0 6.9 %collective-permute-start.103 = (f32[10,1,512]{2,1,0:T(1,128)S(1)}, f32[10,1,512]{2,1,0:T(1,128)S(1)}, u32[]{:S(2)}, u32[]{:S(2)}) collective-permute-start(f32[10,1,512]{2,1,0:T(1,128)S(1)} %get-tuple-element.37), channel_id=1, source_target_pairs={{1,0},{2,1},{3,2},{4,3},{5,4},{6,5},{7,6},{8,7},{9,8},{10,9},{11,1... | collective-permute-start | bytes 61448 | tf_op jit(solution)/shard_map/ppermute | solution.py:24
  584.5 8.0 %collective-permute-start.106 = (f32[10,1,512]{2,1,0:T(1,128)S(1)}, f32[10,1,512]{2,1,0:T(1,128)S(1)}, u32[]{:S(2)}, u32[]{:S(2)}) collective-permute-start(f32[10,1,512]{2,1,0:T(1,128)S(1)} %get-tuple-element.34), channel_id=1, source_target_pairs={{0,1},{1,2},{2,3},{3,4},{4,5},{5,6},{6,7},{7,8},{8,9},{9,10},{10,1... | collective-permute-start | bytes 61448 | tf_op jit(solution)/shard_map/ppermute | solution.py:22
  586.4 6.9 %collective-permute-start.107 = (f32[10,1,512]{2,1,0:T(1,128)S(1)}, f32[10,1,512]{2,1,0:T(1,128)S(1)}, u32[]{:S(2)}, u32[]{:S(2)}) collective-permute-start(f32[10,1,512]{2,1,0:T(1,128)S(1)} %get-tuple-element.35), channel_id=1, source_target_pairs={{1,0},{2,1},{3,2},{4,3},{5,4},{6,5},{7,6},{8,7},{9,8},{10,9},{11,1... | collective-permute-start | bytes 61448 | tf_op jit(solution)/shard_map/ppermute | solution.py:24
  602.9 8.0 %collective-permute-start.110 = (f32[10,1,512]{2,1,0:T(1,128)S(1)}, f32[10,1,512]{2,1,0:T(1,128)S(1)}, u32[]{:S(2)}, u32[]{:S(2)}) collective-permute-start(f32[10,1,512]{2,1,0:T(1,128)S(1)} %get-tuple-element.32), channel_id=1, source_target_pairs={{0,1},{1,2},{2,3},{3,4},{4,5},{5,6},{6,7},{7,8},{8,9},{9,10},{10,1... | collective-permute-start | bytes 61448 | tf_op jit(solution)/shard_map/ppermute | solution.py:22
  604.9 6.9 %collective-permute-start.111 = (f32[10,1,512]{2,1,0:T(1,128)S(1)}, f32[10,1,512]{2,1,0:T(1,128)S(1)}, u32[]{:S(2)}, u32[]{:S(2)}) collective-permute-start(f32[10,1,512]{2,1,0:T(1,128)S(1)} %get-tuple-element.33), channel_id=1, source_target_pairs={{1,0},{2,1},{3,2},{4,3},{5,4},{6,5},{7,6},{8,7},{9,8},{10,9},{11,1... | collective-permute-start | bytes 61448 | tf_op jit(solution)/shard_map/ppermute | solution.py:24
  (78 other events, 1021.7 us)
where the time goes:
time: 619 us; the launch traced here: 614 us
  starting transfers between devices  362 us (58%)
  local copies, waits for them, and re-layouts  111 us (18%)
  other arithmetic  74.9 us (12%)
  waiting for transfers between devices  62.7 us (10%)
    ppermute x56, starting transfers between devices, with_halo(): lax.ppermute(head, axis, [((i + 1) % count, i) for i in range(ends)])  219 us
    ppermute x56, starting transfers between devices, with_halo(): lax.ppermute(tail, axis, [(i, (i + 1) % count) for i in range(ends)])  143 us
    reshape x3, local copies, waits for them, and re-layouts, restrict(): field.reshape(z_cells // 2, 2, y_cells // 2, 2, x_cells // 2, 2)  77.6 us
    ppermute x56, waiting for transfers between devices, with_halo(): lax.ppermute(head, axis, [((i + 1) % count, i) for i in range(ends)])  62.6 us
    reduce_sum x8, other arithmetic, restrict(): field.reshape(z_cells // 2, 2, y_cells // 2, 2, x_cells // 2, 2)  33.3 us
    concatenate x31, other arithmetic, with_halo(): jnp.concatenate([lax.ppermute(tail, axis, [(i, (i + 1) % count) for i in...  14.3 us
    add x16, other arithmetic, smooth(): iterate + OMEGA * (source - apply_operator(iterate, padder(iterate), weig...  12.5 us
  transfers between devices with their start and end apart: 112, of which 33 were waited for; matrix products, arithmetic and copies ran while one was open for 23% of the time, Pallas kernels for 0%

commit v1 on v0

v1 whole, which is shorter than its diff:
```python
import functools

import jax
import jax.numpy as jnp
from jax import lax
from jax.experimental import pallas as pl
from jax.experimental.pallas import tpu as pltpu
from jax.sharding import PartitionSpec as P

MESH = pl.DeviceIdType.MESH
F32 = jnp.float32
LN = 128


def windows(lo, hi, rows=8):
    starts = list(range(lo, hi - rows + 1, rows))
    if starts[-1] + rows < hi:
        starts.append(hi - rows)
    return starts


def lane_of(v):
    return lax.broadcasted_iota(jnp.int32, v.shape, v.ndim - 1)


def next_x(v):
    r = pltpu.roll(v, LN - 1, axis=2)
    if v.shape[0] == 1:
        return r
    carry = jnp.concatenate([r[1:], r[:1]], axis=0)
    return jnp.where(lane_of(v) == LN - 1, carry, r)


def prev_x(v):
    r = pltpu.roll(v, 1, axis=2)
    if v.shape[0] == 1:
        return r
    carry = jnp.concatenate([r[-1:], r[:-1]], axis=0)
    return jnp.where(lane_of(v) == 0, carry, r)


def x_index(v):
    tile = lax.broadcasted_iota(jnp.int32, v.shape, 0)
    return tile * LN + lane_of(v)


def neighbour_sum(a, w, z, y, n):
    wx, wy, wz = w[0], w[1], w[2]
    ys = pl.ds(y, n)
    v = a[z, :, ys, :]
    wxc = wx[z, :, ys, :]
    acc = wxc * next_x(v) + prev_x(wxc * v)
    acc += wy[z, :, ys, :] * a[z, :, pl.ds(y + 1, n), :]
    acc += wy[z, :, pl.ds(y - 1, n), :] * a[z, :, pl.ds(y - 1, n), :]
    acc += wz[z, :, ys, :] * a[z + 1, :, ys, :]
    acc += wz[z - 1, :, ys, :] * a[z - 1, :, ys, :]
    return v, acc


def sweep(a, out, w, s, zs, yr):
    def step(z, c):
        for y in windows(*yr):
            v, acc = neighbour_sum(a, w, z, y, 8)
            ys = pl.ds(y, 8)
            out[z, :, ys, :] = 0.2 * v + w[3][z, :, ys, :] * (s[z, :, ys, :] + acc)
        return c

    lax.fori_loop(zs[0], zs[1], step, 0)


def defect(a, out, w, s, zs, yr):
    def step(z, c):
        for y in windows(*yr):
            v, acc = neighbour_sum(a, w, z, y, 8)
            ys = pl.ds(y, 8)
            out[z, :, ys, :] = s[z, :, ys, :] + (acc - w[4][z, :, ys, :] * v)
        return c

    lax.fori_loop(zs[0], zs[1], step, 0)


def weights(b, w, zs, yr, nx):
    wx, wy, wz, d, tot = w

    def step(z, c):
        for y in windows(yr[0] - 1, yr[1]):
            ys = pl.ds(y, 8)
            wy[z, :, ys, :] = 0.5 * (b[z, :, ys, :] + b[z, :, pl.ds(y + 1, 8), :])
        for y in windows(*yr):
            ys = pl.ds(y, 8)
            v = b[z, :, ys, :]
            x = x_index(v)
            up = jnp.where(x >= nx - 1, 0.0, next_x(v))
            down = jnp.where(x == 0, 0.0, prev_x(v))
            above = b[z + 1, :, ys, :]
            wx[z, :, ys, :] = jnp.where(x >= nx - 1, 0.0, 0.5 * (v + up))
            wz[z, :, ys, :] = 0.5 * (v + above)
            beside = b[z, :, pl.ds(y + 1, 8), :] + b[z, :, pl.ds(y - 1, 8), :]
            total = 3.0 * v + 0.5 * ((up + down) + beside + (above + b[z - 1, :, ys, :]))
            tot[z, :, ys, :] = total
            d[z, :, ys, :] = jnp.where(v > 0.0, 0.8 / total, 0.0)
        return c

    lax.fori_loop(zs[0], zs[1], step, 0)
    z = zs[0] - 1
    for y in windows(*yr):
        ys = pl.ds(y, 8)
        wz[z, :, ys, :] = 0.5 * (b[z, :, ys, :] + b[z + 1, :, ys, :])


def first_sweep(s, out, w, zs, yr):
    def step(z, c):
        for y in windows(*yr):
            ys = pl.ds(y, 8)
            out[z, :, ys, :] = w[3][z, :, ys, :] * s[z, :, ys, :]
        return c

    lax.fori_loop(zs[0], zs[1], step, 0)


def take(v, index):
    flat = v.reshape(-1, LN)
    return jnp.take_along_axis(flat, index(lax.broadcasted_iota(jnp.int32, flat.shape, 1)), axis=1).reshape(v.shape)


def coarsen(f, out, z_f, y_f, z_c, y_c, nz, ny, scale):
    rows = min(ny, 8)

    def step(k, c):
        for y in windows(0, ny, rows):
            even = pl.ds(y_f + 2 * y, rows, stride=2)
            odd = pl.ds(y_f + 2 * y + 1, rows, stride=2)
            z = z_f + 2 * k
            v = (f[z, :, even, :] + f[z, :, odd, :]) + (f[z + 1, :, even, :] + f[z + 1, :, odd, :])
            if scale != 1.0:
                v = v * scale
            v = v + pltpu.roll(v, LN - 1, axis=2)
            g = take(v, lambda j: lax.rem(2 * j, LN))
            low = lax.broadcasted_iota(jnp.int32, (rows, LN), 1) < LN // 2
            tiles = v.shape[0]
            for t in range(max(1, tiles // 2)):
                high = g[2 * t + 1] if tiles > 1 else jnp.zeros((rows, LN), F32)
                out[z_c + k, t, pl.ds(y_c + y, rows), :] = jnp.where(low, g[2 * t], high)
        return c

    lax.fori_loop(0, nz, step, 0)


def spread(e, out, z_c, y_c, z_o, y_o, nz, ny, tiles):
    def step(k, c):
        for y in windows(0, ny):
            v = e[z_c + k, :, pl.ds(y_c + y, 8), :]
            parts = [take(v, lambda j: j // 2)]
            if tiles > 1:
                parts.append(take(v, lambda j: LN // 2 + j // 2))
            for t in range(tiles):
                g = parts[t % 2][t // 2]
                out[z_o + k, t, pl.ds(y_o + 2 * y, 8, stride=2), :] = g
                out[z_o + k, t, pl.ds(y_o + 2 * y + 1, 8, stride=2), :] = g
        return c

    lax.fori_loop(0, nz, step, 0)


def add_spread(u, pe, out, z0, nz, yr):
    def step(k, c):
        for y in windows(*yr):
            ys = pl.ds(y, 8)
            p = pe[k, :, ys, :]
            out[z0 + 2 * k, :, ys, :] = u[z0 + 2 * k, :, ys, :] + p
            out[z0 + 2 * k + 1, :, ys, :] = u[z0 + 2 * k + 1, :, ys, :] + p
        return c

    lax.fori_loop(0, nz // 2, step, 0)


def kernel(ng, nw, nx, rhs, den, p_out, r_out,
           sb0, w0a, w0b, w0c, w0d, w0e, va, vb, vc, pe0,
           b1, s1, w1a, w1b, w1c, w1d, w1e, v1a, v1b, v1c, pe1,
           sub2, b2, s2, w2a, w2b, w2c, w2d, w2e, v2a, v2b, v2c, pe2,
           own3, b3, s3, w3a, w3b, w3c, w3d, w3e, e3a, e3b,
           in_sem, out_sem, ssem, rsem, gsem, grsem):
    gz, xy = lax.axis_index("gz"), lax.axis_index("xy")
    w0 = (w0a, w0b, w0c, w0d, w0e)
    w1 = (w1a, w1b, w1c, w1d, w1e)
    w2 = (w2a, w2b, w2c, w2d, w2e)
    w3 = (w3a, w3b, w3c, w3d, w3e)
    b0, s0 = sb0.at[1], sb0.at[0]
    H0, H1, H2, Y3 = 3, 7, 4, 12

    loads = []
    for t in range(4):
        for i, (src, dst) in enumerate(((den, b0), (rhs, s0))):
            cp = pltpu.make_async_copy(
                src.at[:, :, pl.ds(LN * t, LN)], dst.at[pl.ds(H0, 8), t, pl.ds(H0, 32), :], in_sem.at[i, t]
            )
            cp.start()
            loads.append(cp)

    def clear(ref, zs, ys):
        shape = (zs[1] - zs[0], ref.shape[-3], ys[1] - ys[0], LN)
        if len(ref.shape) == 5:
            for k in range(ref.shape[0]):
                ref[k, zs[0]:zs[1], :, ys[0]:ys[1], :] = jnp.zeros(shape, F32)
        else:
            ref[zs[0]:zs[1], :, ys[0]:ys[1], :] = jnp.zeros(shape, F32)

    for ref, h, z, y, reach in ((sb0, H0, 8, 32, 1), (vb, H0, 8, 32, 1), (b1, H1, 4, 16, 2), (s1, H1, 4, 16, 2),
                                (sub2, H2, 2, 8, 2)):
        top, rows = 2 * h + z, 2 * h + y

        @pl.when(gz < reach)
        def _(ref=ref, h=h, rows=rows):
            clear(ref, (0, h), (0, rows))

        @pl.when(gz >= ng - reach)
        def _(ref=ref, h=h, z=z, top=top, rows=rows):
            clear(ref, (h + z, top), (0, rows))

        @pl.when(xy == 0)
        def _(ref=ref, h=h, top=top):
            clear(ref, (0, top), (0, h))

        @pl.when(xy == nw - 1)
        def _(ref=ref, h=h, y=y, top=top, rows=rows):
            clear(ref, (0, top), (h + y, rows))

    for ref in (b3, s3):
        @pl.when(xy < 3)
        def _(ref=ref):
            clear(ref, (0, ng), (0, Y3))

        @pl.when(xy >= nw - 3)
        def _(ref=ref):
            clear(ref, (0, ng), (Y3 + 4, 32))

    for ref in (e3a, e3b):
        clear(ref, (0, 3), (0, 32))
        clear(ref, (3 + ng, 6 + ng), (0, 32))

    def inside(a, b):
        conds = []
        if a:
            conds += [gz + a >= 0, gz + a < ng]
        if b:
            conds += [xy + b >= 0, xy + b < nw]
        return functools.reduce(jnp.logical_and, conds)

    barrier = pltpu.get_barrier_semaphore()

    def greet(to_other):
        def body(k, c):
            for b in range(-3, 4):
                ok = jnp.logical_and(xy + b >= 0, xy + b < nw)
                if b == 0:
                    ok = jnp.logical_and(ok, k != gz)

                @pl.when(ok)
                def _(b=b):
                    to_other(k, b)
            return c

        lax.fori_loop(0, ng, body, 0)

    greet(lambda k, b: pl.semaphore_signal(barrier, inc=1, device_id=(k, xy + b), device_id_type=MESH))
    columns = 1 + jnp.minimum(xy, 3) + jnp.minimum(nw - 1 - xy, 3)
    pl.semaphore_wait(barrier, ng * columns - 1)
    for cp in loads:
        cp.wait()

    used = [0]

    def exchange(moves):
        copies = []
        for a, b, ref, src, dst in moves:
            i = used[0]
            used[0] += 1
            cp = pltpu.make_async_remote_copy(
                src_ref=ref.at[src], dst_ref=ref.at[dst], send_sem=ssem.at[i], recv_sem=rsem.at[i],
                device_id=(gz + a, xy + b), device_id_type=MESH,
            )

            @pl.when(inside(a, b))
            def _(cp=cp):
                cp.start()

            copies.append((a, b, cp))

        def wait_recv():
            for a, b, cp in copies:
                @pl.when(inside(-a, -b))
                def _(cp=cp):
                    cp.wait_recv()

        def wait_send():
            for a, b, cp in copies:
                @pl.when(inside(a, b))
                def _(cp=cp):
                    cp.wait_send()

        return wait_recv, wait_send

    def span(shift, own, h, lo_skip, width):
        if shift == 0:
            return h, h + own
        if shift > 0:
            return max(h - width, h - shift * own), min(h - lo_skip, h - (shift - 1) * own)
        return max(h + own + lo_skip, h - shift * own), min(h + own + width, h + (1 - shift) * own)

    def move(ref, a, b, own, h, wz, wy, lead=(), skip=0):
        z0, z1 = span(a, own[0], h, skip if b == 0 else 0, wz)
        y0, y1 = span(b, own[1], h, skip if a == 0 else 0, wy)
        dst = lead + (pl.ds(z0, z1 - z0), slice(None), pl.ds(y0, y1 - y0), slice(None))
        src = lead + (pl.ds(z0 + a * own[0], z1 - z0), slice(None), pl.ds(y0 + b * own[1], y1 - y0), slice(None))
        return (a, b, ref, src, dst)

    all2 = (slice(None),)
    o0, o1, o2 = (8, 32), (4, 16), (2, 8)
    signs = (-1, 1)
    moves = [move(sb0, a, 0, o0, H0, 3, 0, (1,)) for a in signs]
    moves += [move(sb0, a, 0, o0, H0, 2, 0, (0,)) for a in signs]
    moves += [move(sb0, 0, b, o0, H0, 0, 3, all2) for b in signs]
    moves += [move(sb0, a, b, o0, H0, 2, 2, all2) for a in signs for b in signs]
    got0, sent0 = exchange(moves)

    coarsen(b0, b1, H0, H0, H1, H1, 4, 16, 1.0)
    moves = [move(b1, a, 0, o1, H1, 7, 0) for a in (-1, 1, -2, 2)]
    moves += [move(b1, 0, b, o1, H1, 0, 7) for b in signs]
    moves += [move(b1, a, b, o1, H1, 7, 6) for a in signs for b in signs]
    moves += [move(b1, a, b, o1, H1, 6, 2) for a in (-2, 2) for b in signs]
    gotb1, sentb1 = exchange(moves)
    coarsen(b1, b2, H1, H1, H2, H2, 2, 8, 1.0)
    coarsen(b2, own3.at[0], H2, H2, 0, 0, 1, 4, 1.0)

    got0()
    weights(b0, w0, (1, 13), (1, 37), nx)
    first_sweep(s0, va, w0, (1, 13), (1, 37))
    sweep(va, vb, w0, s0, (3, 11), (2, 36))
    sweep(va, vb, w0, s0, (2, 3), (3, 35))
    sweep(va, vb, w0, s0, (11, 12), (3, 35))
    defect(vb, vc, w0, s0, (3, 11), (3, 35))
    coarsen(vc, s1, H0, H0, H1, H1, 4, 16, 4.0)

    moves = [move(s1, a, 0, o1, H1, 6, 0) for a in (-1, 1, -2, 2)]
    moves += [move(s1, 0, b, o1, H1, 0, 6) for b in signs]
    moves += [move(s1, a, b, o1, H1, 6, 5) for a in signs for b in signs]
    moves += [move(s1, a, b, o1, H1, 5, 1) for a in (-2, 2) for b in signs]
    gots1, sents1 = exchange(moves)

    moves = [move(vb, a, 0, o0, H0, 3, 0, skip=1) for a in signs]
    moves += [move(vb, 0, b, o0, H0, 0, 3, skip=1) for b in signs]
    moves += [move(vb, a, b, o0, H0, 2, 2) for a in signs for b in signs]
    gotu0, sentu0 = exchange(moves)

    def gather(own, ref, g):
        for b in (0, 1, -1, 2, -2, 3, -3):
            rows = pl.ds(Y3 - 4 * b, 4)

            @pl.when(jnp.logical_and(xy + b >= 0, xy + b < nw))
            def _(b=b, rows=rows):
                def body(k, c):
                    def go():
                        pltpu.make_async_remote_copy(
                            src_ref=own.at[0], dst_ref=ref.at[gz, :, rows, :], send_sem=gsem.at[g, b + 3],
                            recv_sem=grsem.at[g, b + 3], device_id=(k, xy + b), device_id_type=MESH,
                        ).start()

                    if b == 0:
                        pl.when(k != gz)(go)
                    else:
                        go()
                    return c

                lax.fori_loop(0, ng, body, 0)

        def wait(sems, sign):
            for b in (0, 1, -1, 2, -2, 3, -3):
                planes = ng - 1 if b == 0 else ng
                part = ref.at[pl.ds(0, planes), :, pl.ds(Y3 - 4 * b, 4), :]

                @pl.when(jnp.logical_and(xy + sign * b >= 0, xy + sign * b < nw))
                def _(b=b, part=part):
                    pltpu.make_async_copy(part, part, sems.at[g, b + 3]).wait()

        return lambda: wait(grsem, -1), lambda: wait(gsem, 1)

    b3[gz, :, pl.ds(Y3, 4), :] = own3[0, 0]
    gotb3, sentb3 = gather(own3.at[0], b3, 0)
    gotb1()
    weights(b1, w1, (1, 17), (1, 29), nx // 2)
    coarsen(b1, b2, 1, 1, 1, 1, 8, 14, 1.0)
    weights(b2, w2, (2, 8), (2, 14), nx // 4)

    gots1()
    first_sweep(s1, v1a, w1, (1, 17), (1, 29))
    sweep(v1a, v1b, w1, s1, (2, 16), (2, 28))
    defect(v1b, v1c, w1, s1, (3, 15), (3, 27))
    coarsen(v1c, s2, 3, 3, 2, 2, 6, 12, 4.0)
    first_sweep(s2, v2a, w2, (2, 8), (2, 14))
    sweep(v2a, v2b, w2, s2, (3, 7), (3, 13))
    defect(v2b, v2c, w2, s2, (4, 6), (4, 12))
    coarsen(v2c, own3.at[1], H2, H2, 0, 0, 1, 4, 4.0)

    s3[gz, :, pl.ds(Y3, 4), :] = own3[1, 0]
    gots3, sents3 = gather(own3.at[1], s3, 1)

    for i, ref in enumerate((b2, s2, v2b)):
        sub2[i, pl.ds(H2, 2), :, pl.ds(H2, 8), :] = ref[pl.ds(H2, 2), :, pl.ds(H2, 8), :]
    moves = [move(sub2, a, b, o2, H2, 4, 4, all2) for a in range(-2, 3) for b in (-1, 0, 1) if (a, b) != (0, 0)]
    gotsub, sentsub = exchange(moves)

    gotb3()
    R = (2, 26)
    n = R[1] - R[0]
    v = b3[:, 0, pl.ds(R[0], n), :]
    x = lane_of(v)
    zero = jnp.zeros((1, n, LN), F32)
    up = jnp.where(x >= nx // 8 - 1, 0.0, pltpu.roll(v, LN - 1, axis=2))
    down = jnp.where(x == 0, 0.0, pltpu.roll(v, 1, axis=2))
    above = jnp.concatenate([v[1:], zero], axis=0)
    below = jnp.concatenate([zero, v[:-1]], axis=0)
    north, south = b3[:, 0, pl.ds(R[0] + 1, n), :], b3[:, 0, pl.ds(R[0] - 1, n), :]
    w3a[:, pl.ds(R[0], n), :] = jnp.where(x >= nx // 8 - 1, 0.0, 0.5 * (v + up))
    w3b[:, pl.ds(R[0], n), :] = 0.5 * (v + north)
    w3e[:, pl.ds(R[0], n), :] = 0.5 * (v + south)
    w3c[pl.ds(1, ng), pl.ds(R[0], n), :] = 0.5 * (v + above)
    w3c[pl.ds(0, 1), pl.ds(R[0], n), :] = zero
    total = 3.0 * v + 0.5 * ((up + down) + (north + south) + (above + below))
    w3d[:, pl.ds(R[0], n), :] = jnp.where(v > 0.0, 0.8 / total, 0.0)
    gots3()
    e3a[pl.ds(3, ng), 0, pl.ds(R[0], n), :] = w3d[:, pl.ds(R[0], n), :] * s3[:, 0, pl.ds(R[0], n), :]
    a, out = e3a, e3b
    for lo, n in ((3, 22), (3, 22), (6, 16), (6, 16), (6, 16), (6, 16), (10, 8)):
        rows = pl.ds(lo, n)
        v = a[pl.ds(3, ng), 0, rows, :]
        wx = w3a[:, rows, :]
        acc = wx * pltpu.roll(v, LN - 1, axis=2) + pltpu.roll(wx * v, 1, axis=2)
        acc += w3b[:, rows, :] * a[pl.ds(3, ng), 0, pl.ds(lo + 1, n), :]
        acc += w3e[:, rows, :] * a[pl.ds(3, ng), 0, pl.ds(lo - 1, n), :]
        acc += w3c[pl.ds(1, ng), rows, :] * a[pl.ds(4, ng), 0, rows, :]
        acc += w3c[pl.ds(0, ng), rows, :] * a[pl.ds(2, ng), 0, rows, :]
        out[pl.ds(3, ng), 0, rows, :] = 0.2 * v + w3d[:, rows, :] * (s3[:, 0, rows, :] + acc)
        a, out = out, a

    gotsub()
    weights(sub2.at[0], w2, (1, 9), (1, 15), nx // 4)
    spread(a, pe2, gz + 1, 10, 0, 0, 5, 8, 1)
    add_spread(sub2.at[2], pe2, v2a, 0, 10, (0, 16))
    sweep(v2a, v2b, w2, sub2.at[1], (1, 9), (1, 15))
    sweep(v2b, v2a, w2, sub2.at[1], (2, 8), (2, 14))

    spread(v2a, pe1, 2, 2, 0, 3, 6, 12, 2)
    add_spread(v1b, pe1, v1a, 3, 12, (3, 27))
    sweep(v1a, v1c, w1, s1, (4, 14), (4, 26))
    sweep(v1c, v1a, w1, s1, (5, 13), (5, 25))

    spread(v1a, pe0, 5, 5, 0, 0, 8, 20, 4)
    gotu0()

    def add0(k, c):
        for y in windows(0, 38):
            va[k, :, pl.ds(y, 8), :] = vb[k, :, pl.ds(y, 8), :] + pe0[(k + 1) // 2, :, pl.ds(y + 1, 8), :]
        return c

    lax.fori_loop(0, 14, add0, 0)
    sweep(va, vc, w0, s0, (1, 13), (1, 37))
    sweep(vc, va, w0, s0, (2, 12), (2, 36))
    stores = []

    def store(src, dst, i):
        for t in range(4):
            cp = pltpu.make_async_copy(
                src.at[pl.ds(H0, 8), t, pl.ds(H0, 32), :], dst.at[:, :, pl.ds(LN * t, LN)], out_sem.at[i, t]
            )
            cp.start()
            stores.append(cp)

    store(va, p_out, 0)
    defect(va, vc, w0, s0, (3, 11), (3, 35))
    store(vc, r_out, 1)
    for wait in (sent0, sentb1, sents1, sentu0, sentb3, sents3, sentsub):
        wait()
    for cp in stores:
        cp.wait()


def solution(mesh):
    ng, nw = mesh.shape["gz"], mesh.shape["xy"]

    def block(rhs, den):
        nx = rhs.shape[2]
        f0 = pltpu.VMEM((14, 4, 40, LN), F32)
        f1 = pltpu.VMEM((18, 2, 32, LN), F32)
        f2 = pltpu.VMEM((10, 1, 16, LN), F32)
        g3 = pltpu.VMEM((ng, 1, 32, LN), F32)
        w3 = pltpu.VMEM((ng, 32, LN), F32)
        return pl.pallas_call(
            functools.partial(kernel, ng, nw, nx),
            out_shape=[jax.ShapeDtypeStruct(rhs.shape, F32)] * 2,
            in_specs=[pl.BlockSpec(memory_space=pl.ANY)] * 2,
            out_specs=[pl.BlockSpec(memory_space=pl.ANY)] * 2,
            scratch_shapes=[pltpu.VMEM((2, 14, 4, 40, LN), F32)] + [f0] * 8 + [pltpu.VMEM((8, 4, 40, LN), F32)]
            + [f1] * 10 + [pltpu.VMEM((6, 2, 32, LN), F32)]
            + [pltpu.VMEM((3, 10, 1, 16, LN), F32)] + [f2] * 10 + [pltpu.VMEM((5, 1, 16, LN), F32)]
            + [pltpu.VMEM((2, 1, 1, 4, LN), F32), g3, g3, w3, w3, pltpu.VMEM((ng + 1, 32, LN), F32), w3, w3]
            + [pltpu.VMEM((ng + 6, 1, 32, LN), F32)] * 2
            + [pltpu.SemaphoreType.DMA((2, 4))] * 2
            + [pltpu.SemaphoreType.DMA((64,))] * 2
            + [pltpu.SemaphoreType.DMA((2, 7))] * 2,
            compiler_params=pltpu.CompilerParams(
                collective_id=0, has_side_effects=True, vmem_limit_bytes=50 * 2**20
            ),
        )(rhs, den)

    spec = P("gz", "xy", None)
    return jax.shard_map(block, mesh=mesh, in_specs=(spec, spec), out_specs=(spec, spec), check_vma=False)
```

time: 619 us -> 58.5 us (0.09)
  starting transfers between devices: 362 us -> 0 us
  local copies, waits for them, and re-layouts: 111 us -> 3.66 us
  other arithmetic: 74.9 us -> 0 us
  waiting for transfers between devices: 62.7 us -> 0 us
  Pallas kernels: 0 us -> 54 us
    ppermute x112 -> x0, starting transfers between devices: 362 us -> none  [the longest x56 219 us: with_halo(): lax.ppermute(head, axis, [((i + 1) % count, i) for i in range(ends)])]
    reshape x8 -> x0, local copies, waits for them, and re-layouts: 87.2 us -> none  [the longest x3 77.6 us: restrict(): field.reshape(z_cells // 2, 2, y_cells // 2, 2, x_cells // 2, 2)]
    ppermute x112 -> x0, waiting for transfers between devices: 62.7 us -> none  [the longest x56 62.6 us: with_halo(): lax.ppermute(head, axis, [((i + 1) % count, i) for i in range(ends)])]
    pallas_call x0 -> x1, Pallas kernels: none -> 54 us  [block(): pl.pallas_call(functools.partial(kernel, ng, nw, nx), out_shape=[jax.Shap...]
    reduce_sum x8 -> x0, other arithmetic: 33.3 us -> none  [restrict(): field.reshape(z_cells // 2, 2, y_cells // 2, 2, x_cells // 2, 2)]
    add x19 -> x0, other arithmetic: 15.4 us -> none  [the longest x16 12.5 us: smooth(): iterate + OMEGA * (source - apply_operator(iterate, padder(iterate), weig...]
    concatenate x31 -> x0, other arithmetic: 14.3 us -> none  [with_halo(): jnp.concatenate([lax.ppermute(tail, axis, [(i, (i + 1) % count) for i in...]
    broadcast_in_dim x14 -> x0, local copies, waits for them, and re-layouts: 12.2 us -> none  [the longest x10 11.5 us: prolong(): return jnp.repeat(jnp.repeat(jnp.repeat(field, 2, 0), 2, 1), 2, 2)]
  transfers between devices with their start and end apart: 112 -> 0, of which waited for: 33 -> 0; matrix products, arithmetic and copies ran while one was open for 23% -> 0% of each run, Pallas kernels for 0% -> 0%
where the time goes in v1:
time: 58.5 us; the launch traced here: 58.3 us
  Pallas kernels  54 us (92%)
  local copies, waits for them, and re-layouts  3.66 us (6%)
  between operations  0.65 us (1%)
    pallas_call x1, Pallas kernels, block(): pl.pallas_call(functools.partial(kernel, ng, nw, nx), out_shape=[jax.Shap...  54 us
    unnamed x6, local copies, waits for them, and re-layouts  3.66 us

profile of v1, /device:TPU:25, one launch (start us, length us, event | category | flops | bytes accessed | tf_op | source)
XLA Modules:
  0.0 58.3 jit_solution(16827982327156310850)
XLA Ops:
  0.6 0.0 copy-start
  0.6 1.0 %copy-done = f32[8,32,512]{2,1,0:T(8,128)S(1)} copy-done((f32[8,32,512]{2,1,0:T(8,128)S(1)}, f32[8,32,512]{2,1,0:T(8,128)}, u32[]{:S(2)}) %copy-start) | copy-done | bytes 524312
  1.7 0.0 copy-start.1
  1.7 1.0 %copy-done.1 = f32[8,32,512]{2,1,0:T(8,128)S(1)} copy-done((f32[8,32,512]{2,1,0:T(8,128)S(1)}, f32[8,32,512]{2,1,0:T(8,128)}, u32[]{:S(2)}) %copy-start.1) | copy-done | bytes 524312
  2.7 54.0 %shard_map.41 = (f32[8,32,512]{2,1,0:T(8,128)S(1)}, f32[8,32,512]{2,1,0:T(8,128)S(1)}) custom-call(f32[8,32,512]{2,1,0:T(8,128)S(1)} %copy-done, f32[8,32,512]{2,1,0:T(8,128)S(1)} %copy-done.1), custom_call_target="tpu_custom_call" | custom-call | tf_op jit(solution)/shard_map/pallas_call | solution.py:497
  56.7 0.8 %copy.6 = f32[8,32,512]{2,1,0:T(8,128)} copy(f32[8,32,512]{2,1,0:T(8,128)S(1)} %get-tuple-element.4) | data formatting | bytes 1048576
  57.5 0.8 %copy.7 = f32[8,32,512]{2,1,0:T(8,128)} copy(f32[8,32,512]{2,1,0:T(8,128)S(1)} %get-tuple-element.5) | data formatting | bytes 1048576
Async XLA Ops:
  0.6 1.0 %copy-start = (f32[8,32,512]{2,1,0:T(8,128)S(1)}, f32[8,32,512]{2,1,0:T(8,128)}, u32[]{:S(2)}) copy-start(f32[8,32,512]{2,1,0:T(8,128)} %rhs.1) | copy-start | bytes 1572868
  1.7 1.0 %copy-start.1 = (f32[8,32,512]{2,1,0:T(8,128)S(1)}, f32[8,32,512]{2,1,0:T(8,128)}, u32[]{:S(2)}) copy-start(f32[8,32,512]{2,1,0:T(8,128)} %den.1) | copy-start | bytes 1572868

commit v2 on v1

--- a/solution.py
+++ b/solution.py
@@ -57,51 +57,80 @@
     return v, acc
 
 
+PLANES = {4: 4, 2: 4, 1: 16}
+
+
+def planes(zs, body, tiles):
+    n, u = zs[1] - zs[0], min(PLANES[tiles], zs[1] - zs[0])
+
+    def run(z0, k):
+        todo = []
+        for i in range(k):
+            todo += body(z0 + i)
+        for ref, index, value in todo:
+            ref[index] = value
+
+    if n // u > 1:
+        def step(k, c):
+            run(zs[0] + k * u, u)
+            return c
+
+        lax.fori_loop(0, n // u, step, 0)
+    else:
+        run(zs[0], u)
+    if n % u:
+        run(zs[1] - n % u, n % u)
+
+
 def sweep(a, out, w, s, zs, yr):
-    def step(z, c):
+    def body(z):
+        todo = []
         for y in windows(*yr):
             v, acc = neighbour_sum(a, w, z, y, 8)
-            ys = pl.ds(y, 8)
-            out[z, :, ys, :] = 0.2 * v + w[3][z, :, ys, :] * (s[z, :, ys, :] + acc)
-        return c
-
-    lax.fori_loop(zs[0], zs[1], step, 0)
+            at = (z, slice(None), pl.ds(y, 8), slice(None))
+            todo.append((out, at, 0.2 * v + w[3][at] * (s[at] + acc)))
+        return todo
+
+    planes(zs, body, a.shape[1])
 
 
 def defect(a, out, w, s, zs, yr):
-    def step(z, c):
+    def body(z):
+        todo = []
         for y in windows(*yr):
             v, acc = neighbour_sum(a, w, z, y, 8)
-            ys = pl.ds(y, 8)
-            out[z, :, ys, :] = s[z, :, ys, :] + (acc - w[4][z, :, ys, :] * v)
-        return c
-
-    lax.fori_loop(zs[0], zs[1], step, 0)
+            at = (z, slice(None), pl.ds(y, 8), slice(None))
+            todo.append((out, at, s[at] + (acc - w[4][at] * v)))
+        return todo
+
+    planes(zs, body, a.shape[1])
 
 
 def weights(b, w, zs, yr, nx):
     wx, wy, wz, d, tot = w
 
-    def step(z, c):
+    def body(z):
+        todo = []
         for y in windows(yr[0] - 1, yr[1]):
-            ys = pl.ds(y, 8)
-            wy[z, :, ys, :] = 0.5 * (b[z, :, ys, :] + b[z, :, pl.ds(y + 1, 8), :])
+            at = (z, slice(None), pl.ds(y, 8), slice(None))
+            todo.append((wy, at, 0.5 * (b[at] + b[z, :, pl.ds(y + 1, 8), :])))
         for y in windows(*yr):
             ys = pl.ds(y, 8)
-            v = b[z, :, ys, :]
+            at = (z, slice(None), ys, slice(None))
+            v = b[at]
             x = x_index(v)
             up = jnp.where(x >= nx - 1, 0.0, next_x(v))
             down = jnp.where(x == 0, 0.0, prev_x(v))
             above = b[z + 1, :, ys, :]
-            wx[z, :, ys, :] = jnp.where(x >= nx - 1, 0.0, 0.5 * (v + up))
-            wz[z, :, ys, :] = 0.5 * (v + above)
+            todo.append((wx, at, jnp.where(x >= nx - 1, 0.0, 0.5 * (v + up))))
+            todo.append((wz, at, 0.5 * (v + above)))
             beside = b[z, :, pl.ds(y + 1, 8), :] + b[z, :, pl.ds(y - 1, 8), :]
             total = 3.0 * v + 0.5 * ((up + down) + beside + (above + b[z - 1, :, ys, :]))
-            tot[z, :, ys, :] = total
-            d[z, :, ys, :] = jnp.where(v > 0.0, 0.8 / total, 0.0)
-        return c
-
-    lax.fori_loop(zs[0], zs[1], step, 0)
+            todo.append((tot, at, total))
+            todo.append((d, at, jnp.where(v > 0.0, 0.8 / total, 0.0)))
+        return todo
+
+    planes(zs, body, b.shape[1])
     z = zs[0] - 1
     for y in windows(*yr):
         ys = pl.ds(y, 8)
@@ -109,13 +138,14 @@
 
 
 def first_sweep(s, out, w, zs, yr):
-    def step(z, c):
+    def body(z):
+        todo = []
         for y in windows(*yr):
-            ys = pl.ds(y, 8)
-            out[z, :, ys, :] = w[3][z, :, ys, :] * s[z, :, ys, :]
-        return c
-
-    lax.fori_loop(zs[0], zs[1], step, 0)
+            at = (z, slice(None), pl.ds(y, 8), slice(None))
+            todo.append((out, at, w[3][at] * s[at]))
+        return todo
+
+    planes(zs, body, s.shape[1])
 
 
 def take(v, index):
@@ -126,7 +156,8 @@
 def coarsen(f, out, z_f, y_f, z_c, y_c, nz, ny, scale):
     rows = min(ny, 8)
 
-    def step(k, c):
+    def body(k):
+        todo = []
         for y in windows(0, ny, rows):
             even = pl.ds(y_f + 2 * y, rows, stride=2)
             odd = pl.ds(y_f + 2 * y + 1, rows, stride=2)
@@ -140,38 +171,41 @@
             tiles = v.shape[0]
             for t in range(max(1, tiles // 2)):
                 high = g[2 * t + 1] if tiles > 1 else jnp.zeros((rows, LN), F32)
-                out[z_c + k, t, pl.ds(y_c + y, rows), :] = jnp.where(low, g[2 * t], high)
-        return c
-
-    lax.fori_loop(0, nz, step, 0)
+                todo.append((out, (z_c + k, t, pl.ds(y_c + y, rows), slice(None)), jnp.where(low, g[2 * t], high)))
+        return todo
+
+    planes((0, nz), body, max(1, f.shape[1] // 2))
 
 
 def spread(e, out, z_c, y_c, z_o, y_o, nz, ny, tiles):
-    def step(k, c):
+    def body(k):
+        todo = []
         for y in windows(0, ny):
             v = e[z_c + k, :, pl.ds(y_c + y, 8), :]
             parts = [take(v, lambda j: j // 2)]
             if tiles > 1:
                 parts.append(take(v, lambda j: LN // 2 + j // 2))
             for t in range(tiles):
-                g = parts[t % 2][t // 2]
-                out[z_o + k, t, pl.ds(y_o + 2 * y, 8, stride=2), :] = g
-                out[z_o + k, t, pl.ds(y_o + 2 * y + 1, 8, stride=2), :] = g
-        return c
-
-    lax.fori_loop(0, nz, step, 0)
+                for i in range(2):
+                    at = (z_o + k, t, pl.ds(y_o + 2 * y + i, 8, stride=2), slice(None))
+                    todo.append((out, at, parts[t % 2][t // 2]))
+        return todo
+
+    planes((0, nz), body, max(1, tiles // 2))
 
 
 def add_spread(u, pe, out, z0, nz, yr):
-    def step(k, c):
+    def body(k):
+        todo = []
         for y in windows(*yr):
             ys = pl.ds(y, 8)
             p = pe[k, :, ys, :]
-            out[z0 + 2 * k, :, ys, :] = u[z0 + 2 * k, :, ys, :] + p
-            out[z0 + 2 * k + 1, :, ys, :] = u[z0 + 2 * k + 1, :, ys, :] + p
-        return c
-
-    lax.fori_loop(0, nz // 2, step, 0)
+            for i in range(2):
+                at = (z0 + 2 * k + i, slice(None), ys, slice(None))
+                todo.append((out, at, u[at] + p))
+        return todo
+
+    planes((0, nz // 2), body, u.shape[1])
 
 
 def kernel(ng, nw, nx, rhs, den, p_out, r_out,

time: 58.5 us -> 47.9 us (0.82)
  Pallas kernels: 54 us -> 43.3 us
    pallas_call x1, Pallas kernels: 54 us -> 43.3 us  [block(): pl.pallas_call(functools.partial(kernel, ng, nw, nx), out_shape=[jax.Shap...]
where the time goes in v2:
time: 47.9 us; the launch traced here: 47.7 us
  Pallas kernels  43.3 us (90%)
  local copies, waits for them, and re-layouts  3.66 us (8%)
  between operations  0.65 us (1%)
    pallas_call x1, Pallas kernels, block(): pl.pallas_call(functools.partial(kernel, ng, nw, nx), out_shape=[jax.Shap...  43.3 us
    unnamed x6, local copies, waits for them, and re-layouts  3.66 us

profile of v2, /device:TPU:25, one launch (start us, length us, event | category | flops | bytes accessed | tf_op | source)
XLA Modules:
  0.0 47.7 jit_solution(13395845732459053741)
XLA Ops:
  0.6 0.0 copy-start
  0.6 1.0 %copy-done = f32[8,32,512]{2,1,0:T(8,128)S(1)} copy-done((f32[8,32,512]{2,1,0:T(8,128)S(1)}, f32[8,32,512]{2,1,0:T(8,128)}, u32[]{:S(2)}) %copy-start) | copy-done | bytes 524312
  1.7 0.0 copy-start.1
  1.7 1.0 %copy-done.1 = f32[8,32,512]{2,1,0:T(8,128)S(1)} copy-done((f32[8,32,512]{2,1,0:T(8,128)S(1)}, f32[8,32,512]{2,1,0:T(8,128)}, u32[]{:S(2)}) %copy-start.1) | copy-done | bytes 524312
  2.7 43.3 %shard_map.41 = (f32[8,32,512]{2,1,0:T(8,128)S(1)}, f32[8,32,512]{2,1,0:T(8,128)S(1)}) custom-call(f32[8,32,512]{2,1,0:T(8,128)S(1)} %copy-done, f32[8,32,512]{2,1,0:T(8,128)S(1)} %copy-done.1), custom_call_target="tpu_custom_call" | custom-call | tf_op jit(solution)/shard_map/pallas_call | solution.py:531
  46.1 0.8 %copy.6 = f32[8,32,512]{2,1,0:T(8,128)} copy(f32[8,32,512]{2,1,0:T(8,128)S(1)} %get-tuple-element.4) | data formatting | bytes 1048576
  46.9 0.8 %copy.7 = f32[8,32,512]{2,1,0:T(8,128)} copy(f32[8,32,512]{2,1,0:T(8,128)S(1)} %get-tuple-element.5) | data formatting | bytes 1048576
Async XLA Ops:
  0.6 1.0 %copy-start = (f32[8,32,512]{2,1,0:T(8,128)S(1)}, f32[8,32,512]{2,1,0:T(8,128)}, u32[]{:S(2)}) copy-start(f32[8,32,512]{2,1,0:T(8,128)} %rhs.1) | copy-start | bytes 1572868
  1.7 1.0 %copy-start.1 = (f32[8,32,512]{2,1,0:T(8,128)S(1)}, f32[8,32,512]{2,1,0:T(8,128)}, u32[]{:S(2)}) copy-start(f32[8,32,512]{2,1,0:T(8,128)} %den.1) | copy-start | bytes 1572868

commit v3 on v2

--- a/solution.py
+++ b/solution.py
@@ -259,14 +259,13 @@
         def _(ref=ref, h=h, y=y, top=top, rows=rows):
             clear(ref, (0, top), (h + y, rows))
 
-    for ref in (b3, s3):
-        @pl.when(xy < 3)
-        def _(ref=ref):
-            clear(ref, (0, ng), (0, Y3))
-
-        @pl.when(xy >= nw - 3)
-        def _(ref=ref):
-            clear(ref, (0, ng), (Y3 + 4, 32))
+    @pl.when(xy < 3)
+    def _():
+        clear(s3, (0, ng), (0, Y3))
+
+    @pl.when(xy >= nw - 3)
+    def _():
+        clear(s3, (0, ng), (Y3 + 4, 32))
 
     for ref in (e3a, e3b):
         clear(ref, (0, 3), (0, 32))
@@ -282,21 +281,18 @@
 
     barrier = pltpu.get_barrier_semaphore()
 
-    def greet(to_other):
+    def reach(start):
         def body(k, c):
             for b in range(-3, 4):
                 ok = jnp.logical_and(xy + b >= 0, xy + b < nw)
                 if b == 0:
                     ok = jnp.logical_and(ok, k != gz)
-
-                @pl.when(ok)
-                def _(b=b):
-                    to_other(k, b)
+                pl.when(ok)(functools.partial(start, k, b))
             return c
 
         lax.fori_loop(0, ng, body, 0)
 
-    greet(lambda k, b: pl.semaphore_signal(barrier, inc=1, device_id=(k, xy + b), device_id_type=MESH))
+    reach(lambda k, b: pl.semaphore_signal(barrier, inc=1, device_id=(k, xy + b), device_id_type=MESH))
     columns = 1 + jnp.minimum(xy, 3) + jnp.minimum(nw - 1 - xy, 3)
     pl.semaphore_wait(barrier, ng * columns - 1)
     for cp in loads:
@@ -364,7 +360,7 @@
     moves += [move(b1, a, b, o1, H1, 6, 2) for a in (-2, 2) for b in signs]
     gotb1, sentb1 = exchange(moves)
     coarsen(b1, b2, H1, H1, H2, H2, 2, 8, 1.0)
-    coarsen(b2, own3.at[0], H2, H2, 0, 0, 1, 4, 1.0)
+    coarsen(b2, own3.at[1], H2, H2, 0, 0, 1, 4, 1.0)
 
     got0()
     weights(b0, w0, (1, 13), (1, 37), nx)
@@ -381,51 +377,18 @@
     moves += [move(s1, a, b, o1, H1, 5, 1) for a in (-2, 2) for b in signs]
     gots1, sents1 = exchange(moves)
 
+    gotb1()
+    weights(b1, w1, (1, 17), (1, 29), nx // 2)
+    coarsen(b1, b2, 1, 1, 1, 1, 8, 14, 1.0)
+    weights(b2, w2, (2, 8), (2, 14), nx // 4)
+
+    gots1()
+
     moves = [move(vb, a, 0, o0, H0, 3, 0, skip=1) for a in signs]
     moves += [move(vb, 0, b, o0, H0, 0, 3, skip=1) for b in signs]
     moves += [move(vb, a, b, o0, H0, 2, 2) for a in signs for b in signs]
     gotu0, sentu0 = exchange(moves)
 
-    def gather(own, ref, g):
-        for b in (0, 1, -1, 2, -2, 3, -3):
-            rows = pl.ds(Y3 - 4 * b, 4)
-
-            @pl.when(jnp.logical_and(xy + b >= 0, xy + b < nw))
-            def _(b=b, rows=rows):
-                def body(k, c):
-                    def go():
-                        pltpu.make_async_remote_copy(
-                            src_ref=own.at[0], dst_ref=ref.at[gz, :, rows, :], send_sem=gsem.at[g, b + 3],
-                            recv_sem=grsem.at[g, b + 3], device_id=(k, xy + b), device_id_type=MESH,
-                        ).start()
-
-                    if b == 0:
-                        pl.when(k != gz)(go)
-                    else:
-                        go()
-                    return c
-
-                lax.fori_loop(0, ng, body, 0)
-
-        def wait(sems, sign):
-            for b in (0, 1, -1, 2, -2, 3, -3):
-                planes = ng - 1 if b == 0 else ng
-                part = ref.at[pl.ds(0, planes), :, pl.ds(Y3 - 4 * b, 4), :]
-
-                @pl.when(jnp.logical_and(xy + sign * b >= 0, xy + sign * b < nw))
-                def _(b=b, part=part):
-                    pltpu.make_async_copy(part, part, sems.at[g, b + 3]).wait()
-
-        return lambda: wait(grsem, -1), lambda: wait(gsem, 1)
-
-    b3[gz, :, pl.ds(Y3, 4), :] = own3[0, 0]
-    gotb3, sentb3 = gather(own3.at[0], b3, 0)
-    gotb1()
-    weights(b1, w1, (1, 17), (1, 29), nx // 2)
-    coarsen(b1, b2, 1, 1, 1, 1, 8, 14, 1.0)
-    weights(b2, w2, (2, 8), (2, 14), nx // 4)
-
-    gots1()
     first_sweep(s1, v1a, w1, (1, 17), (1, 29))
     sweep(v1a, v1b, w1, s1, (2, 16), (2, 28))
     defect(v1b, v1c, w1, s1, (3, 15), (3, 27))
@@ -433,17 +396,41 @@
     first_sweep(s2, v2a, w2, (2, 8), (2, 14))
     sweep(v2a, v2b, w2, s2, (3, 7), (3, 13))
     defect(v2b, v2c, w2, s2, (4, 6), (4, 12))
-    coarsen(v2c, own3.at[1], H2, H2, 0, 0, 1, 4, 4.0)
-
-    s3[gz, :, pl.ds(Y3, 4), :] = own3[1, 0]
-    gots3, sents3 = gather(own3.at[1], s3, 1)
+    coarsen(v2c, own3.at[0], H2, H2, 0, 0, 1, 4, 4.0)
+
+    mine = own3[0, 0, 0]
+    own3[2, 0, 0] = jnp.where(lane_of(mine) < LN // 2, mine, pltpu.roll(own3[1, 0, 0], LN // 2, axis=1))
+    s3[gz, :, pl.ds(Y3, 4), :] = own3[2, 0]
+    sides = (0, 1, -1, 2, -2, 3, -3)
+
+    def send3(k, b):
+        pltpu.make_async_remote_copy(
+            src_ref=own3.at[2, 0], dst_ref=s3.at[gz, :, pl.ds(Y3 - 4 * b, 4), :], send_sem=gsem.at[b + 3],
+            recv_sem=grsem.at[b + 3], device_id=(k, xy + b), device_id_type=MESH,
+        ).start()
+
+    reach(send3)
+
+    def wait3(sems, sign):
+        for b in sides:
+            part = s3.at[pl.ds(0, ng - 1 if b == 0 else ng), :, pl.ds(Y3 - 4 * b, 4), :]
+
+            @pl.when(jnp.logical_and(xy + sign * b >= 0, xy + sign * b < nw))
+            def _(b=b, part=part):
+                pltpu.make_async_copy(part, part, sems.at[b + 3]).wait()
+
+    gots3, sents3 = lambda: wait3(grsem, -1), lambda: wait3(gsem, 1)
 
     for i, ref in enumerate((b2, s2, v2b)):
         sub2[i, pl.ds(H2, 2), :, pl.ds(H2, 8), :] = ref[pl.ds(H2, 2), :, pl.ds(H2, 8), :]
     moves = [move(sub2, a, b, o2, H2, 4, 4, all2) for a in range(-2, 3) for b in (-1, 0, 1) if (a, b) != (0, 0)]
     gotsub, sentsub = exchange(moves)
 
-    gotb3()
+    gots3()
+    v = s3[:, 0, pl.ds(0, 28), :]
+    low = lane_of(v) < LN // 2
+    b3[:, 0, pl.ds(0, 28), :] = jnp.where(low, pltpu.roll(v, LN // 2, axis=2), 0.0)
+    s3[:, 0, pl.ds(0, 28), :] = jnp.where(low, v, 0.0)
     R = (2, 26)
     n = R[1] - R[0]
     v = b3[:, 0, pl.ds(R[0], n), :]
@@ -461,7 +448,6 @@
     w3c[pl.ds(0, 1), pl.ds(R[0], n), :] = zero
     total = 3.0 * v + 0.5 * ((up + down) + (north + south) + (above + below))
     w3d[:, pl.ds(R[0], n), :] = jnp.where(v > 0.0, 0.8 / total, 0.0)
-    gots3()
     e3a[pl.ds(3, ng), 0, pl.ds(R[0], n), :] = w3d[:, pl.ds(R[0], n), :] * s3[:, 0, pl.ds(R[0], n), :]
     a, out = e3a, e3b
     for lo, n in ((3, 22), (3, 22), (6, 16), (6, 16), (6, 16), (6, 16), (10, 8)):
@@ -491,12 +477,21 @@
     spread(v1a, pe0, 5, 5, 0, 0, 8, 20, 4)
     gotu0()
 
-    def add0(k, c):
-        for y in windows(0, 38):
-            va[k, :, pl.ds(y, 8), :] = vb[k, :, pl.ds(y, 8), :] + pe0[(k + 1) // 2, :, pl.ds(y + 1, 8), :]
-        return c
-
-    lax.fori_loop(0, 14, add0, 0)
+    def add0(fine):
+        def body(k):
+            todo = []
+            for y in windows(0, 38):
+                p = pe0[k, :, pl.ds(y + 1, 8), :]
+                for i in fine:
+                    at = (2 * k + i, slice(None), pl.ds(y, 8), slice(None))
+                    todo.append((va, at, vb[at] + p))
+            return todo
+
+        return body
+
+    planes((0, 1), add0((0,)), 4)
+    planes((1, 7), add0((-1, 0)), 4)
+    planes((7, 8), add0((-1,)), 4)
     sweep(va, vc, w0, s0, (1, 13), (1, 37))
     sweep(vc, va, w0, s0, (2, 12), (2, 36))
     stores = []
@@ -512,7 +507,7 @@
     store(va, p_out, 0)
     defect(va, vc, w0, s0, (3, 11), (3, 35))
     store(vc, r_out, 1)
-    for wait in (sent0, sentb1, sents1, sentu0, sentb3, sents3, sentsub):
+    for wait in (sent0, sentb1, sents1, sentu0, sents3, sentsub):
         wait()
     for cp in stores:
         cp.wait()
@@ -533,14 +528,14 @@
             out_shape=[jax.ShapeDtypeStruct(rhs.shape, F32)] * 2,
             in_specs=[pl.BlockSpec(memory_space=pl.ANY)] * 2,
             out_specs=[pl.BlockSpec(memory_space=pl.ANY)] * 2,
-            scratch_shapes=[pltpu.VMEM((2, 14, 4, 40, LN), F32)] + [f0] * 8 + [pltpu.VMEM((8, 4, 40, LN), F32)]
+            scratch_shapes=[pltpu.VMEM((2, 14, 4, 40, LN), F32)] + [f0] * 8 + [pltpu.VMEM((8, 4, 48, LN), F32)]
             + [f1] * 10 + [pltpu.VMEM((6, 2, 32, LN), F32)]
-            + [pltpu.VMEM((3, 10, 1, 16, LN), F32)] + [f2] * 10 + [pltpu.VMEM((5, 1, 16, LN), F32)]
-            + [pltpu.VMEM((2, 1, 1, 4, LN), F32), g3, g3, w3, w3, pltpu.VMEM((ng + 1, 32, LN), F32), w3, w3]
+            + [pltpu.VMEM((3, 10, 1, 16, LN), F32)] + [f2] * 10 + [pltpu.VMEM((5, 1, 24, LN), F32)]
+            + [pltpu.VMEM((3, 1, 1, 4, LN), F32), g3, g3, w3, w3, pltpu.VMEM((ng + 1, 32, LN), F32), w3, w3]
             + [pltpu.VMEM((ng + 6, 1, 32, LN), F32)] * 2
             + [pltpu.SemaphoreType.DMA((2, 4))] * 2
             + [pltpu.SemaphoreType.DMA((64,))] * 2
-            + [pltpu.SemaphoreType.DMA((2, 7))] * 2,
+            + [pltpu.SemaphoreType.DMA((7,))] * 2,
             compiler_params=pltpu.CompilerParams(
                 collective_id=0, has_side_effects=True, vmem_limit_bytes=50 * 2**20
             ),

time: 47.9 us -> 46.7 us (0.975)
  Pallas kernels: 43.3 us -> 42.2 us
    pallas_call x1, Pallas kernels: 43.3 us -> 42.2 us  [block(): pl.pallas_call(functools.partial(kernel, ng, nw, nx), out_shape=[jax.Shap...]
where the time goes in v3:
time: 46.7 us; the launch traced here: 46.5 us
  Pallas kernels  42.2 us (90%)
  local copies, waits for them, and re-layouts  3.66 us (8%)
  between operations  0.65 us (1%)
    pallas_call x1, Pallas kernels, block(): pl.pallas_call(functools.partial(kernel, ng, nw, nx), out_shape=[jax.Shap...  42.2 us
    unnamed x6, local copies, waits for them, and re-layouts  3.66 us

profile of v3, /device:TPU:25, one launch (start us, length us, event | category | flops | bytes accessed | tf_op | source)
XLA Modules:
  0.0 46.5 jit_solution(8706503918725173127)
XLA Ops:
  0.6 0.0 copy-start
  0.6 1.0 %copy-done = f32[8,32,512]{2,1,0:T(8,128)S(1)} copy-done((f32[8,32,512]{2,1,0:T(8,128)S(1)}, f32[8,32,512]{2,1,0:T(8,128)}, u32[]{:S(2)}) %copy-start) | copy-done | bytes 524312
  1.7 0.0 copy-start.1
  1.7 1.0 %copy-done.1 = f32[8,32,512]{2,1,0:T(8,128)S(1)} copy-done((f32[8,32,512]{2,1,0:T(8,128)S(1)}, f32[8,32,512]{2,1,0:T(8,128)}, u32[]{:S(2)}) %copy-start.1) | copy-done | bytes 524312
  2.7 42.2 %shard_map.41 = (f32[8,32,512]{2,1,0:T(8,128)S(1)}, f32[8,32,512]{2,1,0:T(8,128)S(1)}) custom-call(f32[8,32,512]{2,1,0:T(8,128)S(1)} %copy-done, f32[8,32,512]{2,1,0:T(8,128)S(1)} %copy-done.1), custom_call_target="tpu_custom_call" | custom-call | tf_op jit(solution)/shard_map/pallas_call | solution.py:526
  44.9 0.8 %copy.6 = f32[8,32,512]{2,1,0:T(8,128)} copy(f32[8,32,512]{2,1,0:T(8,128)S(1)} %get-tuple-element.4) | data formatting | bytes 1048576
  45.7 0.8 %copy.7 = f32[8,32,512]{2,1,0:T(8,128)} copy(f32[8,32,512]{2,1,0:T(8,128)S(1)} %get-tuple-element.5) | data formatting | bytes 1048576
Async XLA Ops:
  0.6 1.0 %copy-start = (f32[8,32,512]{2,1,0:T(8,128)S(1)}, f32[8,32,512]{2,1,0:T(8,128)}, u32[]{:S(2)}) copy-start(f32[8,32,512]{2,1,0:T(8,128)} %rhs.1) | copy-start | bytes 1572868
  1.7 1.0 %copy-start.1 = (f32[8,32,512]{2,1,0:T(8,128)S(1)}, f32[8,32,512]{2,1,0:T(8,128)}, u32[]{:S(2)}) copy-start(f32[8,32,512]{2,1,0:T(8,128)} %den.1) | copy-start | bytes 1572868

commit v4 on v3

--- a/solution.py
+++ b/solution.py
@@ -281,9 +281,9 @@
 
     barrier = pltpu.get_barrier_semaphore()
 
-    def reach(start):
+    def reach(start, far=3):
         def body(k, c):
-            for b in range(-3, 4):
+            for b in range(-far, far + 1):
                 ok = jnp.logical_and(xy + b >= 0, xy + b < nw)
                 if b == 0:
                     ok = jnp.logical_and(ok, k != gz)
@@ -292,8 +292,8 @@
 
         lax.fori_loop(0, ng, body, 0)
 
-    reach(lambda k, b: pl.semaphore_signal(barrier, inc=1, device_id=(k, xy + b), device_id_type=MESH))
-    columns = 1 + jnp.minimum(xy, 3) + jnp.minimum(nw - 1 - xy, 3)
+    reach(lambda k, b: pl.semaphore_signal(barrier, inc=1, device_id=(k, xy + b), device_id_type=MESH), 1)
+    columns = 1 + jnp.minimum(xy, 1) + jnp.minimum(nw - 1 - xy, 1)
     pl.semaphore_wait(barrier, ng * columns - 1)
     for cp in loads:
         cp.wait()
@@ -377,17 +377,18 @@
     moves += [move(s1, a, b, o1, H1, 5, 1) for a in (-2, 2) for b in signs]
     gots1, sents1 = exchange(moves)
 
+    moves = [move(vb, a, 0, o0, H0, 3, 0, skip=1) for a in signs]
+    moves += [move(vb, 0, b, o0, H0, 0, 3, skip=1) for b in signs]
+    moves += [move(vb, a, b, o0, H0, 2, 2) for a in signs for b in signs]
+    gotu0, sentu0 = exchange(moves)
+    sent0()
+    sentb1()
     gotb1()
     weights(b1, w1, (1, 17), (1, 29), nx // 2)
     coarsen(b1, b2, 1, 1, 1, 1, 8, 14, 1.0)
     weights(b2, w2, (2, 8), (2, 14), nx // 4)
 
     gots1()
-
-    moves = [move(vb, a, 0, o0, H0, 3, 0, skip=1) for a in signs]
-    moves += [move(vb, 0, b, o0, H0, 0, 3, skip=1) for b in signs]
-    moves += [move(vb, a, b, o0, H0, 2, 2) for a in signs for b in signs]
-    gotu0, sentu0 = exchange(moves)
 
     first_sweep(s1, v1a, w1, (1, 17), (1, 29))
     sweep(v1a, v1b, w1, s1, (2, 16), (2, 28))
@@ -426,6 +427,9 @@
     moves = [move(sub2, a, b, o2, H2, 4, 4, all2) for a in range(-2, 3) for b in (-1, 0, 1) if (a, b) != (0, 0)]
     gotsub, sentsub = exchange(moves)
 
+    sents1()
+    sentu0()
+    sents3()
     gots3()
     v = s3[:, 0, pl.ds(0, 28), :]
     low = lane_of(v) < LN // 2
@@ -507,8 +511,7 @@
     store(va, p_out, 0)
     defect(va, vc, w0, s0, (3, 11), (3, 35))
     store(vc, r_out, 1)
-    for wait in (sent0, sentb1, sents1, sentu0, sents3, sentsub):
-        wait()
+    sentsub()
     for cp in stores:
         cp.wait()
 
@@ -539,7 +542,7 @@
             compiler_params=pltpu.CompilerParams(
                 collective_id=0, has_side_effects=True, vmem_limit_bytes=50 * 2**20
             ),
-        )(rhs, den)
+        )(*(pltpu.with_memory_space_constraint(x, pltpu.HBM) for x in (rhs, den)))
 
     spec = P("gz", "xy", None)
     return jax.shard_map(block, mesh=mesh, in_specs=(spec, spec), out_specs=(spec, spec), check_vma=False)

time: 46.7 us -> 43.5 us (0.931)
  local copies, waits for them, and re-layouts: 3.66 us -> 1.59 us
  Pallas kernels: 42.2 us -> 41.1 us
    unnamed x6 -> x2, local copies, waits for them, and re-layouts: 3.66 us -> 1.59 us
    pallas_call x1, Pallas kernels: 42.2 us -> 41.1 us  [block(): pl.pallas_call(functools.partial(kernel, ng, nw, nx), out_shape=[jax.Shap...]
where the time goes in v4:
time: 43.5 us; the launch traced here: 43.3 us
  Pallas kernels  41.1 us (94%)
  local copies, waits for them, and re-layouts  1.59 us (4%)
  between operations  0.64 us (1%)
    pallas_call x1, Pallas kernels, block(): pl.pallas_call(functools.partial(kernel, ng, nw, nx), out_shape=[jax.Shap...  41.1 us
    unnamed x2, local copies, waits for them, and re-layouts  1.59 us

profile of v4, /device:TPU:25, one launch (start us, length us, event | category | flops | bytes accessed | tf_op | source)
XLA Modules:
  0.0 43.3 jit_solution(3468264912605239839)
XLA Ops:
  0.6 41.1 %shard_map.41 = (f32[8,32,512]{2,1,0:T(8,128)S(1)}, f32[8,32,512]{2,1,0:T(8,128)S(1)}) custom-call(f32[8,32,512]{2,1,0:T(8,128)} %rhs.1, f32[8,32,512]{2,1,0:T(8,128)} %den.1), custom_call_target="tpu_custom_call" | custom-call | tf_op jit(solution)/shard_map/pallas_call | solution.py:529
  41.7 0.8 %copy.6 = f32[8,32,512]{2,1,0:T(8,128)} copy(f32[8,32,512]{2,1,0:T(8,128)S(1)} %get-tuple-element.4) | data formatting | bytes 1048576
  42.5 0.8 %copy.7 = f32[8,32,512]{2,1,0:T(8,128)} copy(f32[8,32,512]{2,1,0:T(8,128)S(1)} %get-tuple-element.5) | data formatting | bytes 1048576

commit v5 on v4

--- a/solution.py
+++ b/solution.py
@@ -57,11 +57,12 @@
     return v, acc
 
 
-PLANES = {4: 4, 2: 4, 1: 16}
+PLANES = {4: 6, 2: 8, 1: 16}
 
 
 def planes(zs, body, tiles):
-    n, u = zs[1] - zs[0], min(PLANES[tiles], zs[1] - zs[0])
+    n = zs[1] - zs[0]
+    u = max(u for u in range(1, PLANES[tiles] + 1) if n % u == 0)
 
     def run(z0, k):
         todo = []
@@ -78,8 +79,6 @@
         lax.fori_loop(0, n // u, step, 0)
     else:
         run(zs[0], u)
-    if n % u:
-        run(zs[1] - n % u, n % u)
 
 
 def sweep(a, out, w, s, zs, yr):
@@ -94,13 +93,14 @@
     planes(zs, body, a.shape[1])
 
 
-def defect(a, out, w, s, zs, yr):
+def defect(a, out, w, s, zs, yr, shift=0):
     def body(z):
         todo = []
         for y in windows(*yr):
             v, acc = neighbour_sum(a, w, z, y, 8)
             at = (z, slice(None), pl.ds(y, 8), slice(None))
-            todo.append((out, at, s[at] + (acc - w[4][at] * v)))
+            to = (z - shift, slice(None), pl.ds(y - shift, 8), slice(None))
+            todo.append((out, to, s[at] + (acc - w[4][at] * v)))
         return todo
 
     planes(zs, body, a.shape[1])
@@ -213,7 +213,7 @@
            b1, s1, w1a, w1b, w1c, w1d, w1e, v1a, v1b, v1c, pe1,
            sub2, b2, s2, w2a, w2b, w2c, w2d, w2e, v2a, v2b, v2c, pe2,
            own3, b3, s3, w3a, w3b, w3c, w3d, w3e, e3a, e3b,
-           in_sem, out_sem, ssem, rsem, gsem, grsem):
+           in_sem, ssem, rsem, gsem, grsem):
     gz, xy = lax.axis_index("gz"), lax.axis_index("xy")
     w0 = (w0a, w0b, w0c, w0d, w0e)
     w1 = (w1a, w1b, w1c, w1d, w1e)
@@ -281,9 +281,9 @@
 
     barrier = pltpu.get_barrier_semaphore()
 
-    def reach(start, far=3):
+    def reach(start):
         def body(k, c):
-            for b in range(-far, far + 1):
+            for b in range(-3, 4):
                 ok = jnp.logical_and(xy + b >= 0, xy + b < nw)
                 if b == 0:
                     ok = jnp.logical_and(ok, k != gz)
@@ -292,9 +292,18 @@
 
         lax.fori_loop(0, ng, body, 0)
 
-    reach(lambda k, b: pl.semaphore_signal(barrier, inc=1, device_id=(k, xy + b), device_id_type=MESH), 1)
-    columns = 1 + jnp.minimum(xy, 1) + jnp.minimum(nw - 1 - xy, 1)
-    pl.semaphore_wait(barrier, ng * columns - 1)
+    greeted = 0
+    for a in (-4, -2, -1, 0, 1, 2, 4):
+        for b in (-1, 0, 1):
+            if (a, b) != (0, 0):
+                ok = inside(a, b)
+
+                @pl.when(ok)
+                def _(a=a, b=b):
+                    pl.semaphore_signal(barrier, inc=1, device_id=(gz + a, xy + b), device_id_type=MESH)
+
+                greeted = greeted + ok.astype(jnp.int32)
+    pl.semaphore_wait(barrier, greeted)
     for cp in loads:
         cp.wait()
 
@@ -498,22 +507,14 @@
     planes((7, 8), add0((-1,)), 4)
     sweep(va, vc, w0, s0, (1, 13), (1, 37))
     sweep(vc, va, w0, s0, (2, 12), (2, 36))
-    stores = []
-
-    def store(src, dst, i):
-        for t in range(4):
-            cp = pltpu.make_async_copy(
-                src.at[pl.ds(H0, 8), t, pl.ds(H0, 32), :], dst.at[:, :, pl.ds(LN * t, LN)], out_sem.at[i, t]
-            )
-            cp.start()
-            stores.append(cp)
-
-    store(va, p_out, 0)
-    defect(va, vc, w0, s0, (3, 11), (3, 35))
-    store(vc, r_out, 1)
+
+    def keep(z):
+        own = (slice(None), pl.ds(H0, 32), slice(None))
+        return [(p_out, (z - H0,), va[(z,) + own])]
+
+    planes((H0, H0 + 8), keep, 4)
+    defect(va, r_out, w0, s0, (3, 11), (3, 35), H0)
     sentsub()
-    for cp in stores:
-        cp.wait()
 
 
 def solution(mesh):
@@ -526,17 +527,17 @@
         f2 = pltpu.VMEM((10, 1, 16, LN), F32)
         g3 = pltpu.VMEM((ng, 1, 32, LN), F32)
         w3 = pltpu.VMEM((ng, 32, LN), F32)
-        return pl.pallas_call(
+        out = pl.pallas_call(
             functools.partial(kernel, ng, nw, nx),
-            out_shape=[jax.ShapeDtypeStruct(rhs.shape, F32)] * 2,
+            out_shape=[jax.ShapeDtypeStruct((8, 4, 32, LN), F32)] * 2,
             in_specs=[pl.BlockSpec(memory_space=pl.ANY)] * 2,
-            out_specs=[pl.BlockSpec(memory_space=pl.ANY)] * 2,
+            out_specs=[pl.BlockSpec(memory_space=pltpu.VMEM)] * 2,
             scratch_shapes=[pltpu.VMEM((2, 14, 4, 40, LN), F32)] + [f0] * 8 + [pltpu.VMEM((8, 4, 48, LN), F32)]
             + [f1] * 10 + [pltpu.VMEM((6, 2, 32, LN), F32)]
             + [pltpu.VMEM((3, 10, 1, 16, LN), F32)] + [f2] * 10 + [pltpu.VMEM((5, 1, 24, LN), F32)]
             + [pltpu.VMEM((3, 1, 1, 4, LN), F32), g3, g3, w3, w3, pltpu.VMEM((ng + 1, 32, LN), F32), w3, w3]
             + [pltpu.VMEM((ng + 6, 1, 32, LN), F32)] * 2
-            + [pltpu.SemaphoreType.DMA((2, 4))] * 2
+            + [pltpu.SemaphoreType.DMA((2, 4))]
             + [pltpu.SemaphoreType.DMA((64,))] * 2
             + [pltpu.SemaphoreType.DMA((7,))] * 2,
             compiler_params=pltpu.CompilerParams(
@@ -544,5 +545,25 @@
             ),
         )(*(pltpu.with_memory_space_constraint(x, pltpu.HBM) for x in (rhs, den)))
 
+        def place(p_ref, r_ref, p_hbm, r_hbm, sem):
+            copies = [
+                pltpu.make_async_copy(src.at[:, t], dst.at[:, :, pl.ds(LN * t, LN)], sem.at[k, t])
+                for k, (src, dst) in enumerate(((p_ref, p_hbm), (r_ref, r_hbm)))
+                for t in range(4)
+            ]
+            for cp in copies:
+                cp.start()
+            for cp in copies:
+                cp.wait()
+
+        return pl.pallas_call(
+            place,
+            out_shape=[jax.ShapeDtypeStruct(rhs.shape, F32)] * 2,
+            in_specs=[pl.BlockSpec(memory_space=pltpu.VMEM)] * 2,
+            out_specs=[pl.BlockSpec(memory_space=pl.ANY)] * 2,
+            scratch_shapes=[pltpu.SemaphoreType.DMA((2, 4))],
+            compiler_params=pltpu.CompilerParams(vmem_limit_bytes=8 * 2**20),
+        )(*out)
+
     spec = P("gz", "xy", None)
     return jax.shard_map(block, mesh=mesh, in_specs=(spec, spec), out_specs=(spec, spec), check_vma=False)

time: 43.5 us -> 41.8 us (0.961)
  local copies, waits for them, and re-layouts: 1.59 us -> 0 us
    unnamed x2 -> x0, local copies, waits for them, and re-layouts: 1.59 us -> none
    pallas_call x1, Pallas kernels: 41.1 us -> 39.9 us  [block(): pl.pallas_call(functools.partial(kernel, ng, nw, nx), out_shape=[jax.Shap...]
    pallas_call x0 -> x1, Pallas kernels: none -> 1.03 us  [block(): pl.pallas_call(place, out_shape=[jax.ShapeDtypeStruct(rhs.shape, F32)] *...]
where the time goes in v5:
time: 41.8 us; the launch traced here: 41.6 us
  Pallas kernels  41 us (98%)
  between operations  0.64 us (2%)
    pallas_call x1, Pallas kernels, block(): pl.pallas_call(functools.partial(kernel, ng, nw, nx), out_shape=[jax.Shap...  39.9 us
    pallas_call x1, Pallas kernels, block(): pl.pallas_call(place, out_shape=[jax.ShapeDtypeStruct(rhs.shape, F32)] *...  1.03 us

profile of v5, /device:TPU:25, one launch (start us, length us, event | category | flops | bytes accessed | tf_op | source)
XLA Modules:
  0.0 41.6 jit_solution(3362048696611800082)
XLA Ops:
  0.6 39.9 %shard_map.41 = (f32[8,4,32,128]{3,2,1,0:T(8,128)S(1)}, f32[8,4,32,128]{3,2,1,0:T(8,128)S(1)}) custom-call(f32[8,32,512]{2,1,0:T(8,128)} %rhs.1, f32[8,32,512]{2,1,0:T(8,128)} %den.1), custom_call_target="tpu_custom_call" | custom-call | tf_op jit(solution)/shard_map/pallas_call | solution.py:530
  40.6 1.0 %shard_map.42 = (f32[8,32,512]{2,1,0:T(8,128)}, f32[8,32,512]{2,1,0:T(8,128)}) custom-call(f32[8,4,32,128]{3,2,1,0:T(8,128)S(1)} %get-tuple-element.4.p_ref, f32[8,4,32,128]{3,2,1,0:T(8,128)S(1)} %get-tuple-element.5.r_ref), custom_call_target="tpu_custom_call" | custom-call | tf_op jit(solution)/shard_map/pallas_call | solution.py:559

commit v6 on v5

--- a/solution.py
+++ b/solution.py
@@ -57,7 +57,7 @@
     return v, acc
 
 
-PLANES = {4: 6, 2: 8, 1: 16}
+PLANES = {4: 14, 2: 16, 1: 16}
 
 
 def planes(zs, body, tiles):
@@ -357,10 +357,10 @@
     o0, o1, o2 = (8, 32), (4, 16), (2, 8)
     signs = (-1, 1)
     moves = [move(sb0, a, 0, o0, H0, 3, 0, (1,)) for a in signs]
-    moves += [move(sb0, a, 0, o0, H0, 2, 0, (0,)) for a in signs]
     moves += [move(sb0, 0, b, o0, H0, 0, 3, all2) for b in signs]
     moves += [move(sb0, a, b, o0, H0, 2, 2, all2) for a in signs for b in signs]
     got0, sent0 = exchange(moves)
+    gots0, sents0 = exchange([move(sb0, a, 0, o0, H0, 2, 0, (0,)) for a in signs])
 
     coarsen(b0, b1, H0, H0, H1, H1, 4, 16, 1.0)
     moves = [move(b1, a, 0, o1, H1, 7, 0) for a in (-1, 1, -2, 2)]
@@ -373,6 +373,7 @@
 
     got0()
     weights(b0, w0, (1, 13), (1, 37), nx)
+    gots0()
     first_sweep(s0, va, w0, (1, 13), (1, 37))
     sweep(va, vb, w0, s0, (3, 11), (2, 36))
     sweep(va, vb, w0, s0, (2, 3), (3, 35))
@@ -391,6 +392,7 @@
     moves += [move(vb, a, b, o0, H0, 2, 2) for a in signs for b in signs]
     gotu0, sentu0 = exchange(moves)
     sent0()
+    sents0()
     sentb1()
     gotb1()
     weights(b1, w1, (1, 17), (1, 29), nx // 2)

time: 41.8 us -> 40.2 us (0.962)
  Pallas kernels: 41 us -> 39.4 us
    pallas_call x1, Pallas kernels: 39.9 us -> 38.3 us  [block(): pl.pallas_call(functools.partial(kernel, ng, nw, nx), out_shape=[jax.Shap...]
where the time goes in v6:
time: 40.2 us; the launch traced here: 40 us
  Pallas kernels  39.4 us (98%)
  between operations  0.64 us (2%)
    pallas_call x1, Pallas kernels, block(): pl.pallas_call(functools.partial(kernel, ng, nw, nx), out_shape=[jax.Shap...  38.3 us
    pallas_call x1, Pallas kernels, block(): pl.pallas_call(place, out_shape=[jax.ShapeDtypeStruct(rhs.shape, F32)] *...  1.03 us

profile of v6, /device:TPU:25, one launch (start us, length us, event | category | flops | bytes accessed | tf_op | source)
XLA Modules:
  0.0 40.0 jit_solution(12586914811420594703)
XLA Ops:
  0.6 38.3 %shard_map.41 = (f32[8,4,32,128]{3,2,1,0:T(8,128)S(1)}, f32[8,4,32,128]{3,2,1,0:T(8,128)S(1)}) custom-call(f32[8,32,512]{2,1,0:T(8,128)} %rhs.1, f32[8,32,512]{2,1,0:T(8,128)} %den.1), custom_call_target="tpu_custom_call" | custom-call | tf_op jit(solution)/shard_map/pallas_call | solution.py:532
  39.0 1.0 %shard_map.42 = (f32[8,32,512]{2,1,0:T(8,128)}, f32[8,32,512]{2,1,0:T(8,128)}) custom-call(f32[8,4,32,128]{3,2,1,0:T(8,128)S(1)} %get-tuple-element.4.p_ref, f32[8,4,32,128]{3,2,1,0:T(8,128)S(1)} %get-tuple-element.5.r_ref), custom_call_target="tpu_custom_call" | custom-call | tf_op jit(solution)/shard_map/pallas_call | solution.py:561

commit v7 on v6

--- a/solution.py
+++ b/solution.py
@@ -363,8 +363,7 @@
     gots0, sents0 = exchange([move(sb0, a, 0, o0, H0, 2, 0, (0,)) for a in signs])
 
     coarsen(b0, b1, H0, H0, H1, H1, 4, 16, 1.0)
-    moves = [move(b1, a, 0, o1, H1, 7, 0) for a in (-1, 1, -2, 2)]
-    moves += [move(b1, 0, b, o1, H1, 0, 7) for b in signs]
+    moves = [move(b1, 0, b, o1, H1, 0, 7) for b in signs]
     moves += [move(b1, a, b, o1, H1, 7, 6) for a in signs for b in signs]
     moves += [move(b1, a, b, o1, H1, 6, 2) for a in (-2, 2) for b in signs]
     gotb1, sentb1 = exchange(moves)
@@ -374,6 +373,7 @@
     got0()
     weights(b0, w0, (1, 13), (1, 37), nx)
     gots0()
+    gotz1, sentz1 = exchange([move(b1, a, 0, o1, H1, 7, 0) for a in (-1, 1, -2, 2)])
     first_sweep(s0, va, w0, (1, 13), (1, 37))
     sweep(va, vb, w0, s0, (3, 11), (2, 36))
     sweep(va, vb, w0, s0, (2, 3), (3, 35))
@@ -381,10 +381,11 @@
     defect(vb, vc, w0, s0, (3, 11), (3, 35))
     coarsen(vc, s1, H0, H0, H1, H1, 4, 16, 4.0)
 
-    moves = [move(s1, a, 0, o1, H1, 6, 0) for a in (-1, 1, -2, 2)]
-    moves += [move(s1, 0, b, o1, H1, 0, 6) for b in signs]
+    moves = [move(s1, a, 0, o1, H1, 6, 0) for a in (-1, 1)]
     moves += [move(s1, a, b, o1, H1, 6, 5) for a in signs for b in signs]
     moves += [move(s1, a, b, o1, H1, 5, 1) for a in (-2, 2) for b in signs]
+    moves += [move(s1, a, 0, o1, H1, 6, 0) for a in (-2, 2)]
+    moves += [move(s1, 0, b, o1, H1, 0, 6) for b in signs]
     gots1, sents1 = exchange(moves)
 
     moves = [move(vb, a, 0, o0, H0, 3, 0, skip=1) for a in signs]
@@ -394,7 +395,9 @@
     sent0()
     sents0()
     sentb1()
+    sentz1()
     gotb1()
+    gotz1()
     weights(b1, w1, (1, 17), (1, 29), nx // 2)
     coarsen(b1, b2, 1, 1, 1, 1, 8, 14, 1.0)
     weights(b2, w2, (2, 8), (2, 14), nx // 4)

time: 40.2 us -> 39.2 us (0.975)
  Pallas kernels: 39.4 us -> 38.3 us
    pallas_call x1, Pallas kernels: 38.3 us -> 37.3 us  [block(): pl.pallas_call(functools.partial(kernel, ng, nw, nx), out_shape=[jax.Shap...]
where the time goes in v7:
time: 39.2 us; the launch traced here: 38.9 us
  Pallas kernels  38.3 us (98%)
  between operations  0.64 us (2%)
    pallas_call x1, Pallas kernels, block(): pl.pallas_call(functools.partial(kernel, ng, nw, nx), out_shape=[jax.Shap...  37.3 us
    pallas_call x1, Pallas kernels, block(): pl.pallas_call(place, out_shape=[jax.ShapeDtypeStruct(rhs.shape, F32)] *...  1.03 us

profile of v7, /device:TPU:25, one launch (start us, length us, event | category | flops | bytes accessed | tf_op | source)
XLA Modules:
  0.0 38.9 jit_solution(7780276547499143665)
XLA Ops:
  0.6 37.3 %shard_map.41 = (f32[8,4,32,128]{3,2,1,0:T(8,128)S(1)}, f32[8,4,32,128]{3,2,1,0:T(8,128)S(1)}) custom-call(f32[8,32,512]{2,1,0:T(8,128)} %rhs.1, f32[8,32,512]{2,1,0:T(8,128)} %den.1), custom_call_target="tpu_custom_call" | custom-call | tf_op jit(solution)/shard_map/pallas_call | solution.py:535
  37.9 1.0 %shard_map.42 = (f32[8,32,512]{2,1,0:T(8,128)}, f32[8,32,512]{2,1,0:T(8,128)}) custom-call(f32[8,4,32,128]{3,2,1,0:T(8,128)S(1)} %get-tuple-element.4.p_ref, f32[8,4,32,128]{3,2,1,0:T(8,128)S(1)} %get-tuple-element.5.r_ref), custom_call_target="tpu_custom_call" | custom-call | tf_op jit(solution)/shard_map/pallas_call | solution.py:564

commit v8 on v7

--- a/solution.py
+++ b/solution.py
@@ -357,8 +357,8 @@
     o0, o1, o2 = (8, 32), (4, 16), (2, 8)
     signs = (-1, 1)
     moves = [move(sb0, a, 0, o0, H0, 3, 0, (1,)) for a in signs]
+    moves += [move(sb0, a, b, o0, H0, 2, 2, all2) for a in signs for b in signs]
     moves += [move(sb0, 0, b, o0, H0, 0, 3, all2) for b in signs]
-    moves += [move(sb0, a, b, o0, H0, 2, 2, all2) for a in signs for b in signs]
     got0, sent0 = exchange(moves)
     gots0, sents0 = exchange([move(sb0, a, 0, o0, H0, 2, 0, (0,)) for a in signs])
 
@@ -388,10 +388,6 @@
     moves += [move(s1, 0, b, o1, H1, 0, 6) for b in signs]
     gots1, sents1 = exchange(moves)
 
-    moves = [move(vb, a, 0, o0, H0, 3, 0, skip=1) for a in signs]
-    moves += [move(vb, 0, b, o0, H0, 0, 3, skip=1) for b in signs]
-    moves += [move(vb, a, b, o0, H0, 2, 2) for a in signs for b in signs]
-    gotu0, sentu0 = exchange(moves)
     sent0()
     sents0()
     sentb1()
@@ -402,6 +398,10 @@
     coarsen(b1, b2, 1, 1, 1, 1, 8, 14, 1.0)
     weights(b2, w2, (2, 8), (2, 14), nx // 4)
 
+    moves = [move(vb, a, 0, o0, H0, 3, 0, skip=1) for a in signs]
+    moves += [move(vb, 0, b, o0, H0, 0, 3, skip=1) for b in signs]
+    moves += [move(vb, a, b, o0, H0, 2, 2) for a in signs for b in signs]
+    gotu0, sentu0 = exchange(moves)
     gots1()
 
     first_sweep(s1, v1a, w1, (1, 17), (1, 29))

time: 39.2 us -> 39.2 us (level)
  no operation moved by 1% of the time
where the time goes in v8:
time: 39.2 us; the launch traced here: 38.8 us
  Pallas kernels  38.1 us (97%)
  between operations  0.64 us (2%)
    pallas_call x1, Pallas kernels, block(): pl.pallas_call(functools.partial(kernel, ng, nw, nx), out_shape=[jax.Shap...  37.1 us
    pallas_call x1, Pallas kernels, block(): pl.pallas_call(place, out_shape=[jax.ShapeDtypeStruct(rhs.shape, F32)] *...  1.03 us

profile of v8, /device:TPU:25, one launch (start us, length us, event | category | flops | bytes accessed | tf_op | source)
XLA Modules:
  0.0 38.8 jit_solution(5082610917971319752)
XLA Ops:
  0.6 37.1 %shard_map.41 = (f32[8,4,32,128]{3,2,1,0:T(8,128)S(1)}, f32[8,4,32,128]{3,2,1,0:T(8,128)S(1)}) custom-call(f32[8,32,512]{2,1,0:T(8,128)} %rhs.1, f32[8,32,512]{2,1,0:T(8,128)} %den.1), custom_call_target="tpu_custom_call" | custom-call | tf_op jit(solution)/shard_map/pallas_call | solution.py:535
  37.7 1.0 %shard_map.42 = (f32[8,32,512]{2,1,0:T(8,128)}, f32[8,32,512]{2,1,0:T(8,128)}) custom-call(f32[8,4,32,128]{3,2,1,0:T(8,128)S(1)} %get-tuple-element.4.p_ref, f32[8,4,32,128]{3,2,1,0:T(8,128)S(1)} %get-tuple-element.5.r_ref), custom_call_target="tpu_custom_call" | custom-call | tf_op jit(solution)/shard_map/pallas_call | solution.py:564
